TPU v7x, 256 devices: a whole 4x4x8 slice. The times are simulated.
256 devices in a mesh: col: 32 (over y, x, core), sec: 8 (over z).
Axes of the slice: x: 4, y: 4, z: 8, core: 2. Of those that a mesh axis runs over, the one named last changes fastest.
Arguments:
- boundaries: bfloat16 [8, 2, 32, 64, 4096], P('sec', None, 'col'), may hold values from -6 to 6
- row_ops: bfloat16 [2, 32, 8, 8, 64, 64], P(None, 'col'), may hold values from -0.25 to 0.25
- ranks: int32 [8, 2, 32], P('sec', None, 'col'), may hold values from 32 to 64, as said below
Outputs:
- canonical: bfloat16 [8, 2, 32, 64, 4096], P('sec', None, 'col')
Inputs may be any that keep to these rules, and one draw needn't show every extreme that they name: `ranks`: for every boundary and column, at least one sector block keeps all 64.
All inputs are finite; a program needn't handle non-finite values.
Results may differ from a plain program's by a relative error of at most 0.0012.
Values may be sent and summed in bfloat16 or wider, within the bound.
A program may use at most 128 MiB of HBM per device.

v0:
```python
import math

import jax
import jax.numpy as jnp
from jax import lax
from jax.sharding import PartitionSpec as P


def passed_along(array, axis, by):
    size = lax.axis_size(axis)
    pairs = [(i, i + by) for i in range(size) if 0 <= i + by < size]
    return lax.ppermute(array, axis, pairs)


def on_device(boundaries, row_ops, ranks):
    high = lax.Precision.HIGHEST
    sectors_here, both, columns, phys, square = boundaries.shape
    block = math.isqrt(square)
    factor = math.sqrt(phys * block)
    my_sector = lax.axis_index("sec") * sectors_here
    ops_mine = lax.dynamic_slice_in_dim(row_ops, my_sector, sectors_here, 3)
    absorbed = jnp.einsum(
        "sbcpx,bcstpq->tbcqx",
        lax.all_gather(boundaries, "sec", axis=0, tiled=True),
        ops_mine,
        preferred_element_type=jnp.float32,
    )
    index = jnp.arange(block, dtype=jnp.int32)
    me_col = lax.axis_index("col")
    steps = lax.axis_size("col")

    def sweep(fields, limits):
        count = fields.shape[1]
        identity = jnp.broadcast_to(
            jnp.eye(block, dtype=jnp.float32), (sectors_here, count, block, block)
        )

        def advance(left):
            field = fields[:, :, 0].reshape(sectors_here, count, phys, block, block)
            mixed = jnp.einsum("sbak,sbpkr->sbpar", left, field, precision=high)
            flat = mixed.reshape(sectors_here, count, phys * block, block)
            gram = jnp.einsum("sbxr,sbxq->sbrq", flat, flat, precision=high)
            lower = jnp.linalg.cholesky(gram)
            ortho = lax.linalg.triangular_solve(
                lower, flat, left_side=False, lower=True, transpose_a=True
            )
            keep = (index[None, None, :] < limits[:, :, 0][:, :, None]).astype(jnp.float32)
            results = [
                (factor * ortho * keep[:, :, None, :])
                .astype(jnp.bfloat16)
                .reshape(sectors_here, count, phys, square)
            ]
            upper = jnp.swapaxes(lower, -1, -2) * keep[:, :, :, None]
            left = upper * lax.rsqrt(jnp.mean(upper * upper, axis=(-2, -1), keepdims=True) + 1e-06)
            return (left, jnp.stack(results, axis=2))

        def turn(step, carry):
            sent, result = carry
            incoming = passed_along(sent, "col", 1)
            entering = jnp.where(step == 0, identity, incoming)

            def working(unused):
                return advance(entering)

            def waiting(unused):
                return (sent, result)

            return lax.cond(me_col == step, working, waiting, 0)

        initial = (identity, jnp.zeros((sectors_here, count, columns, phys, square), jnp.bfloat16))
        _, output = lax.fori_loop(0, steps, turn, initial)
        return output

    upper_half = sweep(absorbed[:, 0:1], ranks[:, 0:1])
    lower_half = sweep(absorbed[:, 1:2], ranks[:, 1:2])
    return jnp.concatenate([upper_half, lower_half], axis=1)


def solution(mesh):
    placed = (
        P("sec", None, "col", None, None),
        P(None, "col", None, None, None, None),
        P("sec", None, "col"),
    )
    return jax.shard_map(
        on_device,
        mesh=mesh,
        in_specs=placed,
        out_specs=P("sec", None, "col", None, None),
        check_vma=False,
    )
```

profile of v0, /device:TPU:31, one launch (start us, length us, event | category | flops | bytes accessed | tf_op | source)
XLA Modules:
  0.0 2073.0 jit_solution(10650367553528306369)
XLA Ops:
  8.7 97.3 %all-gather.2.cloned.1.call-done = bf16[8,2,1,64,4096]{4,3,0,1,2:T(8,128)(2,1)} async-done(((bf16[1,2,1,64,4096]{4,3,0,1,2:T(8,128)(2,1)}), bf16[8,2,1,64,4096]{4,3,0,1,2:T(8,128)(2,1)}) %all-gather.2.cloned.1.call-update) | async-done | bytes 8388624 | tf_op jit(solution)/shard_map/all_gather | solution.py:24
  105.9 5.0 fusion.32
  113.3 1240.0 %while.32 = (s32[]{:T(128)}, f32[1,1,64,64]{2,3,1,0:T(8,128)S(1)}, bf16[1,1,1,64,4096]{4,3,2,1,0:T(8,128)(2,1)}, s32[]{:T(128)}, f32[1,1,1,64,4096]{4,3,2,1,0:T(8,128)}, /*index=5*/s32[1,1,1]{2,1,0:T(1,128)}, s32[]{:T(128)}) while((s32[]{:T(128)}, f32[1,1,64,64]{2,3,1,0:T(8,128)S(1)}, bf16[1,1,1,64,4096]{4,3,2,1,0:T(8,128)(2,1)}, ...), condition=%wide.region_6.9_spmd.clone, body=%wide.region_0.8_spmd.clone.sunk | while | flops 604586304 | bytes 13454140 | solution.py:71
  118.0 3.9 collective-permute-done
  123.3 3.9 collective-permute-done
  134.0 3.9 collective-permute-done
  139.3 3.9 collective-permute-done
  149.9 3.9 collective-permute-done
  155.2 3.9 collective-permute-done
  171.1 3.9 collective-permute-done
  176.5 5.8 collective-permute-done
  183.6 6.0 collective-permute-done
  191.1 6.0 collective-permute-done
  198.5 6.0 collective-permute-done
  205.9 6.0 collective-permute-done
  213.3 6.0 collective-permute-done
  220.7 6.0 collective-permute-done
  228.2 6.0 collective-permute-done
  235.6 6.0 collective-permute-done
  243.0 6.0 collective-permute-done
  250.4 6.0 collective-permute-done
  257.8 6.0 collective-permute-done
  265.3 6.0 collective-permute-done
  272.7 6.0 collective-permute-done
  280.1 6.0 collective-permute-done
  287.5 6.0 collective-permute-done
  294.9 6.0 collective-permute-done
  302.4 6.0 collective-permute-done
  309.8 6.0 collective-permute-done
  317.2 1000.9 %collective-permute-done = f32[1,1,64,64]{3,2,1,0:T(8,128)S(1)} collective-permute-done((f32[1,1,64,64]{3,2,1,0:T(8,128)S(1)}, f32[1,1,64,64]{3,2,1,0:T(8,128)S(1)}, u32[]{:S(2)}, u32[]{:S(2)}) %collective-permute-start) | collective-permute-done | bytes 16416 | tf_op jit(solution)/shard_map/while/body/eval_jaxpr/ppermute | solution.py:12
  1318.2 35.1 %conditional.6 = ((f32[1,1,64,64]{2,3,1,0:T(8,128)S(1)}, bf16[1,1,1,64,4096]{4,3,2,1,0:T(8,128)(2,1)})) conditional(s32[]{:T(128)} %convert_element_type.72, (f32[1,1,64,64]{2,3,1,0:T(8,128)S(1)}, bf16[1,1,1,64,4096]{4,3,2,1,0:T(8,128)(2,1)}) %tuple.96, (s32[]{:T(128)}, f32[1,1,64,64]{3,2,1,0:T(8,128)S(1)}, f32[1,1,64,64]{3,2,1,0:T(8,128)S(1)}, ...), branch_computations={%region_1.1_spmd, %region_2.7_spmd} | conditional | flops 604578112 | bytes 13338993 | solution.py:68
  1329.8 5.8 custom-call.8
  1339.8 4.9 custom-call.9
  1345.4 4.7 fusion.9
  1354.1 709.8 %while.33 = (s32[]{:T(128)}, f32[1,1,64,64]{2,3,1,0:T(8,128)S(1)}, bf16[1,1,1,64,4096]{4,3,2,1,0:T(8,128)(2,1)}, s32[]{:T(128)}, f32[1,1,1,64,4096]{4,3,2,1,0:T(8,128)}, /*index=5*/s32[1,1,1]{2,1,0:T(1,128)}, s32[]{:T(128)}) while((s32[]{:T(128)}, f32[1,1,64,64]{2,3,1,0:T(8,128)S(1)}, bf16[1,1,1,64,4096]{4,3,2,1,0:T(8,128)(2,1)}, ...), condition=%wide.region_11.14_spmd.clone, body=%wide.region_7.13_spmd.clone.sunk | while | flops 604586304 | bytes 13454140 | solution.py:71
  1473.0 4.3 collective-permute-done.1
  1478.7 6.0 collective-permute-done.1
  1486.1 6.0 collective-permute-done.1
  1493.5 6.0 collective-permute-done.1
  1501.0 6.0 collective-permute-done.1
  1508.4 6.0 collective-permute-done.1
  1515.8 6.0 collective-permute-done.1
  1523.2 6.0 collective-permute-done.1
  1530.6 498.5 %collective-permute-done.1 = f32[1,1,64,64]{3,2,1,0:T(8,128)S(1)} collective-permute-done((f32[1,1,64,64]{3,2,1,0:T(8,128)S(1)}, f32[1,1,64,64]{3,2,1,0:T(8,128)S(1)}, u32[]{:S(2)}, u32[]{:S(2)}) %collective-permute-start.1) | collective-permute-done | bytes 16416 | tf_op jit(solution)/shard_map/while/body/eval_jaxpr/ppermute | solution.py:12
  2029.2 34.8 %conditional.7 = ((f32[1,1,64,64]{2,3,1,0:T(8,128)S(1)}, bf16[1,1,1,64,4096]{4,3,2,1,0:T(8,128)(2,1)})) conditional(s32[]{:T(128)} %convert_element_type.74, (f32[1,1,64,64]{2,3,1,0:T(8,128)S(1)}, bf16[1,1,1,64,4096]{4,3,2,1,0:T(8,128)(2,1)}) %tuple.99, (s32[]{:T(128)}, f32[1,1,64,64]{3,2,1,0:T(8,128)S(1)}, f32[1,1,64,64]{3,2,1,0:T(8,128)S(1)}, ...), branch_computations={%region_8.10_spmd, %region_9.0_spmd} | conditional | flops 604578112 | bytes 13338993 | solution.py:68
  2040.8 5.8 custom-call.10
  2050.5 4.9 custom-call.11
  2056.1 4.7 fusion.19
  (385 shorter events, 236.0 us)
Async XLA Ops:
  6.5 99.4 %all-gather.2.cloned.1.call-start = ((), (), s32[]{:S(2)}) async-start(), calls=%async_computation | async-start | bytes 9437184 | tf_op jit(solution)/shard_map/all_gather | solution.py:24
  116.7 5.2 collective-permute-start
  122.0 5.2 collective-permute-start
  132.7 5.2 collective-permute-start
  138.0 5.2 collective-permute-start
  148.6 5.2 collective-permute-start
  153.9 5.2 collective-permute-start
  169.8 5.2 collective-permute-start
  175.1 7.1 collective-permute-start
  182.3 7.3 collective-permute-start
  189.7 7.3 collective-permute-start
  197.2 7.3 collective-permute-start
  204.6 7.3 collective-permute-start
  212.0 7.3 collective-permute-start
  219.4 7.3 collective-permute-start
  226.8 7.3 collective-permute-start
  234.3 7.3 collective-permute-start
  241.7 7.3 collective-permute-start
  249.1 7.3 collective-permute-start
  256.5 7.3 collective-permute-start
  263.9 7.3 collective-permute-start
  271.4 7.3 collective-permute-start
  278.8 7.3 collective-permute-start
  286.2 7.3 collective-permute-start
  293.6 7.3 collective-permute-start
  301.0 7.3 collective-permute-start
  308.5 7.3 collective-permute-start
  315.9 1002.3 %collective-permute-start = (f32[1,1,64,64]{3,2,1,0:T(8,128)S(1)}, f32[1,1,64,64]{3,2,1,0:T(8,128)S(1)}, u32[]{:S(2)}, u32[]{:S(2)}) collective-permute-start(f32[1,1,64,64]{3,2,1,0:T(8,128)S(1)} %copy.45), channel_id=1, source_target_pairs={{0,8},{8,16},{16,24},{24,32},{32,40},{40,48},{48,56},{56,64},{64,7... | collective-permute-start | bytes 49160 | tf_op jit(solution)/shard_map/while/body/eval_jaxpr/ppermute | solution.py:12
  1376.1 5.2 collective-permute-start.1
  1392.0 5.2 collective-permute-start.1
  1397.3 5.2 collective-permute-start.1
  1408.0 5.2 collective-permute-start.1
  1413.3 5.2 collective-permute-start.1
  1423.9 5.2 collective-permute-start.1
  1429.2 5.2 collective-permute-start.1
  1439.8 5.2 collective-permute-start.1
  1445.1 5.2 collective-permute-start.1
  1455.8 5.2 collective-permute-start.1
  1461.1 5.2 collective-permute-start.1
  1471.7 5.6 collective-permute-start.1
  1477.4 7.3 collective-permute-start.1
  1484.8 7.3 collective-permute-start.1
  1492.2 7.3 collective-permute-start.1
  1499.6 7.3 collective-permute-start.1
  1507.1 7.3 collective-permute-start.1
  1514.5 7.3 collective-permute-start.1
  1521.9 7.3 collective-permute-start.1
  1529.3 499.8 %collective-permute-start.1 = (f32[1,1,64,64]{3,2,1,0:T(8,128)S(1)}, f32[1,1,64,64]{3,2,1,0:T(8,128)S(1)}, u32[]{:S(2)}, u32[]{:S(2)}) collective-permute-start(f32[1,1,64,64]{3,2,1,0:T(8,128)S(1)} %copy.46), channel_id=1, source_target_pairs={{0,8},{8,16},{16,24},{24,32},{32,40},{40,48},{48,56},{56,64},{64,7... | collective-permute-start | bytes 49160 | tf_op jit(solution)/shard_map/while/body/eval_jaxpr/ppermute | solution.py:12
  (20 other events, 184.5 us)
Sparse Core Ops, SparseCore 0:
  9.2 96.7 all-gather.1
where the time goes:
time: 2080 us; the launch traced here: 2070 us
  waiting for transfers between devices  1890 us (91%)
  starting transfers between devices  82.6 us (4%)
  other arithmetic  32.2 us (2%)
  matrix products  28.6 us (1%)
  local copies, waits for them, and re-layouts  24.6 us (1%)
    ppermute x64, waiting for transfers between devices, passed_along(): return lax.ppermute(array, axis, pairs)  1790 us
    all_gather x1, waiting for transfers between devices, on_device(): lax.all_gather(boundaries, 'sec', axis=0, tiled=True)  97.3 us
    ppermute x64, starting transfers between devices, passed_along(): return lax.ppermute(array, axis, pairs)  82.6 us
  transfers between devices with their start and end apart: 65, of which 65 were waited for; matrix products, arithmetic and copies ran while one was open for 0% of the time, Pallas kernels for 0%

commit v1 on v0

v1 whole, which is shorter than its diff:
```python
import functools
import math

import jax
import jax.numpy as jnp
from jax import lax
from jax.experimental import pallas as pl
from jax.experimental.pallas import tpu as pltpu
from jax.sharding import PartitionSpec as P

MESH = pl.DeviceIdType.MESH
N = 64
NT = (((1,), (1,)), ((), ()))
NN = (((1,), (0,)), ((), ()))


def dot(a, b, dims):
    return lax.dot_general(a, b, dims, preferred_element_type=jnp.float32)


def split(x):
    hi = x.astype(jnp.bfloat16)
    lo = (x - hi.astype(jnp.float32)).astype(jnp.bfloat16)
    return hi, lo


def factor_pairs(grams):
    count = len(grams)
    rows = [[g[8 * i : 8 * i + 8] for i in range(8)] for g, _ in grams]
    out = [[None] * N for _ in grams]
    wide = (8, 128)
    for p in range(8):
        cols = [{} for _ in grams]
        for n in range(count):
            base = grams[n][1] + 8 * p
            for r in range(p, 8):
                cols[n][r] = [jnp.broadcast_to(rows[n][r][:, base + a : base + a + 1], wide) for a in range(8)]
        for a in range(8):
            for n in range(count):
                pivot = jnp.broadcast_to(cols[n][p][a][a : a + 1, :], wide)
                inverse = 1.0 / pivot
                row = jnp.broadcast_to(rows[n][p][a : a + 1, :], wide)
                out[n][8 * p + a] = row[0:1] * lax.rsqrt(pivot[0:1])
                heads = [jnp.broadcast_to(cols[n][p][b][a : a + 1, :], wide) if b > a else None for b in range(8)]
                for r in range(p, 8):
                    times = cols[n][r][a] * inverse
                    for b in range(a + 1, 8):
                        cols[n][r][b] = cols[n][r][b] - times * heads[b]
                    rows[n][r] = rows[n][r] - times * row
    return [jnp.concatenate(o, 0) for o in out]


def chain_kernel(ranks_ref, at_ref, out_ref, at_hi, at_lo, mixed, l_in, l_out, send_sem, recv_sem):
    me = lax.axis_index("col")
    last = lax.axis_size("col") - 1
    sec = lax.axis_index("sec")
    barrier = pltpu.get_barrier_semaphore()

    @pl.when(me > 0)
    def _():
        pl.semaphore_signal(barrier, inc=1, device_id=(me - 1, sec), device_id_type=MESH)

    for b in range(2):
        for c in range(8):
            hi, lo = split(at_ref[b, 128 * c : 128 * c + 128, :])
            at_hi[b, 128 * c : 128 * c + 128, :] = hi
            at_lo[b, 128 * c : 128 * c + 128, :] = lo

    lane = lax.broadcasted_iota(jnp.int32, (N, 128), 1)
    line = lax.broadcasted_iota(jnp.int32, (N, 128), 0)
    low = lane < N
    place = jnp.where(low, lane, lane - N)
    eye = jnp.where(place == line, 1.0, 0.0).astype(jnp.float32)
    keep = line < jnp.where(low, ranks_ref[0], ranks_ref[1])
    copy = pltpu.make_async_remote_copy(
        src_ref=l_out, dst_ref=l_in, send_sem=send_sem, recv_sem=recv_sem,
        device_id=(jnp.minimum(me + 1, last), sec), device_id_type=MESH,
    )

    @pl.when(me < last)
    def _():
        pl.semaphore_wait(barrier, 1)

    @pl.when(me == 0)
    def _():
        l_in[...] = eye

    @pl.when(me > 0)
    def _():
        copy.wait_recv()

    left = l_in[...]
    turned = pltpu.roll(left, N, 1)
    squares = left * left
    scales = []
    grams = []
    for b in range(2):
        at_low = jnp.where(low, left if b == 0 else turned, 0.0)
        at_high = jnp.where(low, 0.0, turned if b == 0 else left)
        zero = jnp.zeros((N, 128), jnp.bfloat16)
        low_hi, low_lo = split(at_low)
        high_hi, high_lo = split(at_high)

        def diagonal(x, y):
            return jnp.concatenate(
                [jnp.concatenate([x, y, zero, zero], 0), jnp.concatenate([zero, zero, x, y], 0)], 1
            )

        w_hi, w_lo = diagonal(low_hi, high_hi), diagonal(low_lo, high_lo)
        for c in range(8):
            a_hi = at_hi[b, 128 * c : 128 * c + 128, :]
            a_lo = at_lo[b, 128 * c : 128 * c + 128, :]
            x = dot(a_hi, w_hi, NT) + dot(a_lo, w_hi, NT) + dot(a_hi, w_lo, NT)
            hi, lo = split(x)
            mixed[b, 0:128, 256 * c : 256 * c + 256] = hi
            mixed[b, 128:256, 256 * c : 256 * c + 256] = lo
        y = mixed[b]
        g = dot(y, y, NT)
        g = g[0:128] + g[128:256]
        g = g[:, 0:128] + g[:, 128:256]
        even, odd = g[0:N], g[N:]
        total = jnp.sum(jnp.where(low == (b == 0), squares, 0.0), keepdims=True)
        scale = lax.rsqrt(total * (1.0 / (N * N)) + 1e-06)
        scale = jnp.where(me == 0, jnp.ones_like(scale), scale)
        scales.append(scale)
        if b == 0:
            full = (even + pltpu.roll(odd, N, 1)) * (scale * scale)
            grams.append((jnp.where(low, full, eye), 0))
        else:
            full = (pltpu.roll(even, N, 1) + odd) * (scale * scale)
            grams.append((jnp.where(low, eye, full), N))
    first, second = factor_pairs(grams)
    upper = jnp.where(low, first, second)
    l_out[...] = jnp.where(jnp.logical_and(keep, place >= line), upper, 0.0)

    @pl.when(me < last)
    def _():
        copy.start()

    factor = math.sqrt(N * N)
    for b in range(2):
        inverse = second if b else first
        mask = low if b else jnp.logical_not(low)
        rank = ranks_ref[b]
        inverse = jnp.where(jnp.logical_and(mask, line < rank), inverse, 0.0) * (scales[b] * factor)
        other = pltpu.roll(inverse, N, 1)
        pair = jnp.concatenate([inverse, other], 0) if b else jnp.concatenate([other, inverse], 0)
        p_hi, p_lo = split(pair)
        wide_hi = jnp.concatenate([p_hi, p_hi], 1)
        for c in range(8):
            y = mixed[b, :, 256 * c : 256 * c + 256]
            o = dot(wide_hi, y, NN) + dot(p_lo, y[0:128], NN)
            out_ref[b, 128 * c : 128 * c + 128, :] = o.astype(jnp.bfloat16)

    @pl.when(me < last)
    def _():
        copy.wait_send()


def chain(at, ranks):
    vmem = pl.BlockSpec(memory_space=pltpu.VMEM)
    return pl.pallas_call(
        chain_kernel,
        out_shape=jax.ShapeDtypeStruct((2, 1024, 256), jnp.bfloat16),
        in_specs=[pl.BlockSpec(memory_space=pltpu.SMEM), vmem],
        out_specs=vmem,
        scratch_shapes=[
            pltpu.VMEM((2, 1024, 256), jnp.bfloat16),
            pltpu.VMEM((2, 1024, 256), jnp.bfloat16),
            pltpu.VMEM((2, 256, 2048), jnp.bfloat16),
            pltpu.VMEM((N, 128), jnp.float32),
            pltpu.VMEM((N, 128), jnp.float32),
            pltpu.SemaphoreType.DMA,
            pltpu.SemaphoreType.DMA,
        ],
        compiler_params=pltpu.CompilerParams(
            collective_id=0, has_side_effects=True, vmem_limit_bytes=40 * 1024 * 1024
        ),
    )(ranks, at)


def on_device(boundaries, row_ops, ranks):
    my_sector = lax.axis_index("sec")
    ops_mine = lax.dynamic_slice_in_dim(row_ops, my_sector, 1, 3)
    absorbed = jnp.einsum(
        "sbcpx,bcstpq->tbcqx",
        lax.all_gather(boundaries, "sec", axis=0, tiled=True),
        ops_mine,
        preferred_element_type=jnp.float32,
    )
    at = absorbed.reshape(2, 16, 4, N, N).transpose(0, 1, 4, 2, 3).reshape(2, 1024, 256)
    out = chain(at, ranks.reshape(2))
    out = out.reshape(2, 16, N, 4, N).transpose(0, 1, 3, 4, 2)
    return out.reshape(1, 2, 1, N, N * N)


def solution(mesh):
    placed = (
        P("sec", None, "col", None, None),
        P(None, "col", None, None, None, None),
        P("sec", None, "col"),
    )
    return jax.shard_map(
        on_device,
        mesh=mesh,
        in_specs=placed,
        out_specs=P("sec", None, "col", None, None),
        check_vma=False,
    )
```

time: 2080 us -> 369 us (0.18)
  waiting for transfers between devices: 1890 us -> 99.4 us
  Pallas kernels: 0 us -> 223 us
  starting transfers between devices: 82.6 us -> 0.01 us
  other arithmetic: 32.2 us -> 0 us
  matrix products: 28.6 us -> 6.37 us
    ppermute x64 -> x0, waiting for transfers between devices: 1790 us -> none  [passed_along(): return lax.ppermute(array, axis, pairs)]
    pallas_call x0 -> x1, Pallas kernels: none -> 223 us  [chain(): pl.pallas_call(chain_kernel, out_shape=jax.ShapeDtypeStruct((2, 1024, 256...]
    ppermute x64 -> x0, starting transfers between devices: 82.6 us -> none  [passed_along(): return lax.ppermute(array, axis, pairs)]
    another operation x10 -> x0, other arithmetic: 25.5 us -> none  [the longest x6 14.4 us: advance(): lower = jnp.linalg.cholesky(gram)]
  transfers between devices with their start and end apart: 65 -> 1, of which waited for: 65 -> 1; matrix products, arithmetic and copies ran while one was open for 0% -> 0% of each run, Pallas kernels for 0% -> 0%
where the time goes in v1:
time: 369 us
  Pallas kernels  223 us (60%)
  waiting for transfers between devices  99.4 us (27%)
  local copies, waits for them, and re-layouts  26.9 us (7%)
  between operations  13.4 us (4%)
  matrix products  6.37 us (2%)
    pallas_call x1, Pallas kernels, chain(): pl.pallas_call(chain_kernel, out_shape=jax.ShapeDtypeStruct((2, 1024, 256...  223 us
    all_gather x1, waiting for transfers between devices, on_device(): lax.all_gather(boundaries, 'sec', axis=0, tiled=True)  98.7 us
    transpose x2, local copies, waits for them, and re-layouts, on_device(): absorbed.reshape(2, 16, 4, N, N).transpose(0, 1, 4, 2, 3)  9.86 us
  transfers between devices with their start and end apart: 1, of which 1 were waited for; matrix products, arithmetic and copies ran while one was open for 0% of the time, Pallas kernels for 0%

profile of v1, /device:TPU:31, one launch (start us, length us, event | category | flops | bytes accessed | tf_op | source)
XLA Modules:
  0.0 368.8 jit_solution(11201243620943655302)
XLA Ops:
  6.5 0.0 copy-start
  6.5 0.0 all-gather.2.cloned.1.call-start
  6.5 0.7 all-gather.2.cloned.1.call-update
  7.3 98.7 %all-gather.2.cloned.1.call-done = bf16[8,2,1,64,4096]{4,3,0,1,2:T(8,128)(2,1)} async-done(((bf16[1,2,1,64,4096]{4,3,0,1,2:T(8,128)(2,1)}), bf16[8,2,1,64,4096]{4,3,0,1,2:T(8,128)(2,1)}) %all-gather.2.cloned.1.call-update) | async-done | bytes 8388624 | tf_op jit(solution)/shard_map/all_gather | solution.py:187
  105.9 0.0 copy-done
  105.9 6.4 %fusion.2 = f32[2,64,4096]{2,1,0:T(8,128)} fusion(bf16[8,2,1,64,4096]{4,3,0,1,2:T(8,128)(2,1)} %all-gather.2.cloned.1.call-done, bf16[2,1,8,8,64,64]{5,4,3,2,1,0:T(8,128)(2,1)S(1)} %copy-done, s32[]{:T(128)S(6)} %select_n.3), kind=kOutput, calls=%fused_computation.2 | convolution fusion | flops 536870912 | bytes 10747908 | tf_op jit(solution)/shard_map/sbcpx,bcstpq->tbcqx/dot_general | solution.py:185
  112.3 4.6 %transpose.9 = f32[2,16,4,64,64]{4,3,2,1,0:T(8,128)} reshape(f32[2,64,4096]{2,1,0:T(8,128)} %fusion.2) | data formatting | bytes 4194304 | tf_op jit(solution)/shard_map/reshape;sbcpx,bcstpq->tbcqx/transpose | solution.py:191
  116.9 5.3 %copy.6 = f32[2,16,4,64,64]{3,2,4,1,0:T(4,128)} copy(f32[2,16,4,64,64]{4,3,2,1,0:T(8,128)} %transpose.9) | data formatting | bytes 4194304 | tf_op jit(solution)/shard_map/reshape;sbcpx,bcstpq->tbcqx/transpose | solution.py:191
  122.2 0.0 copy-start.2
  122.2 5.3 %reshape.23.at_ref = f32[2,1024,256]{2,1,0:T(8,128)} reshape(f32[2,16,64,4,64]{4,3,2,1,0:T(4,128)} %bitcast.19) | data formatting | bytes 4194304 | tf_op jit(solution)/shard_map/reshape | solution.py:191
  127.4 0.0 copy-done.2
  127.4 0.0 copy-start.1
  127.4 1.6 copy-done.1
  129.0 222.7 %shard_map.37 = bf16[2,1024,256]{2,1,0:T(8,128)(2,1)S(1)} custom-call(s32[2]{0:T(128)S(1)} %bitcast.18, f32[2,1024,256]{2,1,0:T(8,128)S(1)} %copy-done.1), custom_call_target="tpu_custom_call" | custom-call | tf_op jit(solution)/shard_map/pallas_call | solution.py:162
  351.8 1.9 reshape.24
  353.7 4.1 %copy.7 = bf16[2,16,4,64,64]{4,3,2,1,0:T(8,128)(2,1)} copy(bf16[2,16,4,64,64]{3,2,4,1,0:T(4,128)(2,1)} %bitcast.20) | data formatting | bytes 2097152 | tf_op jit(solution)/shard_map/transpose | solution.py:193
  357.8 4.1 %reshape.25 = bf16[1,2,1,64,4096]{4,3,2,1,0:T(8,128)(2,1)} reshape(bf16[2,16,4,64,64]{4,3,2,1,0:T(8,128)(2,1)} %copy.7) | data formatting | bytes 2097152 | tf_op jit(solution)/shard_map/reshape | solution.py:194
Async XLA Ops:
  6.5 99.4 %copy-start = (bf16[2,1,8,8,64,64]{5,4,3,2,1,0:T(8,128)(2,1)S(1)}, bf16[2,1,8,8,64,64]{5,4,3,2,1,0:T(8,128)(2,1)}, u32[]{:S(2)}) copy-start(bf16[2,1,8,8,64,64]{5,4,3,2,1,0:T(8,128)(2,1)} %param.4) | copy-start | bytes 3145732
  6.5 99.4 %all-gather.2.cloned.1.call-start = ((), (), s32[]{:S(2)}) async-start(), calls=%async_computation | async-start | bytes 9437184 | tf_op jit(solution)/shard_map/all_gather | solution.py:187
  122.2 5.3 %copy-start.2 = (s32[1,2,1]{1,2,0:T(1,128)S(1)}, s32[1,2,1]{1,2,0:T(1,128)}, u32[]{:S(2)}) copy-start(s32[1,2,1]{1,2,0:T(1,128)} %param.5) | copy-start | bytes 28
  127.4 1.6 copy-start.1
Sparse Core Ops, SparseCore 0:
  9.2 96.7 all-gather.1

commit v2 on v1

v2 whole, which is shorter than its diff:
```python
import functools
import math

import jax
import jax.numpy as jnp
from jax import lax
from jax.experimental import pallas as pl
from jax.experimental.pallas import tpu as pltpu
from jax.sharding import PartitionSpec as P

MESH = pl.DeviceIdType.MESH
N = 64
NT = (((1,), (1,)), ((), ()))
NN = (((1,), (0,)), ((), ()))


def dot(a, b, dims):
    return lax.dot_general(a, b, dims, preferred_element_type=jnp.float32)


def split(x):
    hi = x.astype(jnp.bfloat16)
    lo = (x - hi.astype(jnp.float32)).astype(jnp.bfloat16)
    return hi, lo


def factor_pairs(grams):
    count = len(grams)
    rows = [[g[8 * i : 8 * i + 8] for i in range(8)] for g, _ in grams]
    out = [[None] * N for _ in grams]
    wide = (8, 128)
    for p in range(8):
        cols = [{} for _ in grams]
        for n in range(count):
            base = grams[n][1] + 8 * p
            for r in range(p, 8):
                cols[n][r] = [jnp.broadcast_to(rows[n][r][:, base + a : base + a + 1], wide) for a in range(8)]
        for a in range(8):
            for n in range(count):
                pivot = jnp.broadcast_to(cols[n][p][a][a : a + 1, :], wide)
                inverse = 1.0 / pivot
                row = jnp.broadcast_to(rows[n][p][a : a + 1, :], wide)
                out[n][8 * p + a] = row[0:1] * lax.rsqrt(pivot[0:1])
                heads = [jnp.broadcast_to(cols[n][p][b][a : a + 1, :], wide) if b > a else None for b in range(8)]
                for r in range(p, 8):
                    times = cols[n][r][a] * inverse
                    for b in range(a + 1, 8):
                        cols[n][r][b] = cols[n][r][b] - times * heads[b]
                    rows[n][r] = rows[n][r] - times * row
    return [jnp.concatenate(o, 0) for o in out]


def patterns():
    lane = lax.broadcasted_iota(jnp.int32, (N, 128), 1)
    line = lax.broadcasted_iota(jnp.int32, (N, 128), 0)
    low = lane < N
    place = jnp.where(low, lane, lane - N)
    eye = jnp.where(place == line, 1.0, 0.0).astype(jnp.float32)
    return line, low, place, eye


def absorb(ops, blocks, acc, q, sectors, first):
    lhs = [ops[q, s] for s in sectors]

    def tile(n, carry):
        at = pl.ds(pl.multiple_of(n * 512, 512), 512)
        total = dot(lhs[0], blocks[q, sectors[0], :, at], NN)
        for left, s in zip(lhs[1:], sectors[1:]):
            total = total + dot(left, blocks[q, s, :, at], NN)
        acc[:, at] = total if first else acc[:, at] + total
        return carry

    lax.fori_loop(0, 8, tile, 0)


def to_columns(acc, rows, at_hi, at_lo, q):
    low = lax.broadcasted_iota(jnp.int32, (32, 128), 1) < N
    for m in range(32):
        v = acc[:, 128 * m : 128 * m + 128]
        w = pltpu.roll(v, N, 1)
        rows[pl.ds(2 * m, 32, stride=N), :] = jnp.where(low, v[0:32], w[32:64])
        rows[pl.ds(2 * m + 1, 32, stride=N), :] = jnp.where(low, w[0:32], v[32:64])
    for t in range(16):
        hi, lo = split(rows[128 * t : 128 * t + 128, :].T)
        c, half = t // 2, 128 * (t % 2)
        at_hi[q, 128 * c : 128 * c + 128, half : half + 128] = hi
        at_lo[q, 128 * c : 128 * c + 128, half : half + 128] = lo


def diagonal(x, y):
    zero = jnp.zeros((N, 128), jnp.bfloat16)
    return jnp.concatenate([jnp.concatenate([x, y, zero, zero], 0), jnp.concatenate([zero, zero, x, y], 0)], 1)


def advance(left, unit, keep, at_hi, at_lo, mixed, q):
    line, low, place, eye = patterns()
    turned = pltpu.roll(left, N, 1)
    low_hi, low_lo = split(jnp.where(low, left, 0.0))
    high_hi, high_lo = split(jnp.where(low, 0.0, turned))
    w_hi, w_lo = diagonal(low_hi, high_hi), diagonal(low_lo, high_lo)
    for c in range(8):
        a_hi = at_hi[q, 128 * c : 128 * c + 128, :]
        a_lo = at_lo[q, 128 * c : 128 * c + 128, :]
        x = dot(a_hi, w_hi, NT) + dot(a_lo, w_hi, NT) + dot(a_hi, w_lo, NT)
        hi, lo = split(x)
        mixed[q, 0:128, 256 * c : 256 * c + 256] = hi
        mixed[q, 128:256, 256 * c : 256 * c + 256] = lo
    y = mixed[q]
    g = dot(y, y, NT)
    g = g[0:128] + g[128:256]
    g = g[:, 0:128] + g[:, 128:256]
    total = jnp.sum(jnp.where(low, left * left, 0.0), keepdims=True)
    scale = lax.rsqrt(total * (1.0 / (N * N)) + 1e-06)
    scale = jnp.where(unit, jnp.ones_like(scale), scale)
    full = (g[0:N] + pltpu.roll(g[N:], N, 1)) * (scale * scale)
    (rows,) = factor_pairs([(jnp.where(low, full, eye), 0)])
    upper = jnp.where(jnp.logical_and(keep, place >= line), rows, 0.0)
    inverse = jnp.where(jnp.logical_or(low, jnp.logical_not(keep)), 0.0, rows) * (scale * float(N))
    return upper, inverse


def results(inverse, mixed, rows, out, q):
    pair = jnp.concatenate([pltpu.roll(inverse, N, 1), inverse], 0)
    p_hi, p_lo = split(pair)
    wide = jnp.concatenate([p_hi, p_hi], 1)
    for c in range(8):
        y = mixed[q, :, 256 * c : 256 * c + 256]
        o = dot(wide, y, NN) + dot(p_lo, y[0:128], NN)
        rows[256 * c : 256 * c + 128, :] = o[:, 0:128].T
        rows[256 * c + 128 : 256 * c + 256, :] = o[:, 128:256].T
    low = lax.broadcasted_iota(jnp.int32, (32, 128), 1) < N
    for m in range(32):
        e = rows[pl.ds(2 * m, 32, stride=N), :]
        d = rows[pl.ds(2 * m + 1, 32, stride=N), :]
        at = slice(128 * m, 128 * m + 128)
        out[q, 0:32, at] = jnp.where(low, e, pltpu.roll(d, N, 1)).astype(jnp.bfloat16)
        out[q, 32:64, at] = jnp.where(low, pltpu.roll(e, N, 1), d).astype(jnp.bfloat16)


def sweep_kernel(
    ops_ref, limit_ref, bnd_ref, out_ref,
    blocks, ops, limits, acc, rows, at_hi, at_lo, mixed, out, l_in, l_out, left_ref,
    part_send, part_recv, own_sem, ring_send, ring_recv, l_send, l_recv, out_send, out_recv, out_own,
):
    me = lax.axis_index("col")
    last = lax.axis_size("col") - 2
    z = lax.axis_index("sec")
    size = lax.axis_size("sec")
    core = lax.rem(me, 2)
    partner = me + 1 - 2 * core
    up, down = lax.rem(z + 1, size), lax.rem(z + size - 1, size)
    has_next = me < last
    has_before = me >= 2

    barrier = pltpu.get_barrier_semaphore()
    for to in ((partner, z), (me, up), (me, down)):
        pl.semaphore_signal(barrier, inc=1, device_id=to, device_id_type=MESH)

    @pl.when(has_before)
    def _():
        pl.semaphore_signal(barrier, inc=1, device_id=(me - 2, z), device_id_type=MESH)

    @pl.when(has_next)
    def _():
        pl.semaphore_wait(barrier, 4)

    @pl.when(jnp.logical_not(has_next))
    def _():
        pl.semaphore_wait(barrier, 3)

    def to_partner(n, source, target):
        return pltpu.make_async_remote_copy(
            src_ref=source, dst_ref=target, send_sem=part_send.at[n], recv_sem=part_recv.at[n],
            device_id=(partner, z), device_id_type=MESH,
        )

    crossing = [
        to_partner(0, bnd_ref.at[0, 1 - core, 0], blocks.at[core, z]),
        to_partner(1, ops_ref.at[1 - core], ops.at[core]),
        to_partner(2, limit_ref.at[1 - core], limits.at[core]),
    ]
    staying = [
        pltpu.make_async_copy(bnd_ref.at[0, core, 0], blocks.at[core, z], own_sem.at[0]),
        pltpu.make_async_copy(ops_ref.at[core], ops.at[core], own_sem.at[1]),
        pltpu.make_async_copy(limit_ref.at[core], limits.at[core], own_sem.at[2]),
    ]
    for copy in crossing + staying:
        copy.start()

    def ring(q, way, d, half):
        block = lax.rem(z + size + (d - 1 if way else 1 - d), size)
        part = blocks.at[q, block, 32 * half : 32 * half + 32]
        return pltpu.make_async_remote_copy(
            src_ref=part, dst_ref=part, send_sem=ring_send.at[q, way, d - 1, half], recv_sem=ring_recv.at[q, way, d - 1, half],
            device_id=(me, down if way else up), device_id_type=MESH,
        )

    def exists(way, d, half):
        return d < 4 or (d == 4 and half == way)

    def begin(q):
        @pl.when(core == q)
        def _():
            staying[0].wait()

        @pl.when(core != q)
        def _():
            crossing[0].wait_recv()

        for half in range(2):
            for way in range(2):
                ring(q, way, 1, half).start()

    def turn(q, d):
        for half in range(2):
            for way in range(2):
                if exists(way, d, half):
                    ring(q, way, d, half).wait_recv()
                    if exists(way, d + 1, half):
                        ring(q, way, d + 1, half).start()

    def sectors(d):
        before, after = lax.rem(z + size - d, size), lax.rem(z + d, size)
        return [z] if d == 0 else [after] if d == 4 else [before, after]

    begin(0)
    for copy in staying[1:]:
        copy.wait()
    for copy in crossing[1:]:
        copy.wait_recv()
    for d in range(5):
        if d > 0:
            turn(0, d)
        if d == 3:
            begin(1)
        absorb(ops, blocks, acc, 0, sectors(d), d == 0)
    turn(1, 1)
    to_columns(acc, rows, at_hi, at_lo, 0)
    absorb(ops, blocks, acc, 1, sectors(0), True)
    absorb(ops, blocks, acc, 1, sectors(1), False)
    for d in range(2, 5):
        turn(1, d)
        absorb(ops, blocks, acc, 1, sectors(d), False)
    to_columns(acc, rows, at_hi, at_lo, 1)

    line, low, place, eye = patterns()
    along = pltpu.make_async_remote_copy(
        src_ref=l_out, dst_ref=l_in, send_sem=l_send, recv_sem=l_recv,
        device_id=(jnp.where(has_next, me + 2, me), z), device_id_type=MESH,
    )

    @pl.when(jnp.logical_not(has_before))
    def _():
        left_ref[...] = eye

    @pl.when(has_before)
    def _():
        along.wait_recv()
        left_ref[...] = l_in[...]

    def keep(q):
        return line.astype(jnp.float32) < limits[q, 0:1, :]

    upper, inverse0 = advance(left_ref[...], jnp.logical_not(has_before), keep(0), at_hi, at_lo, mixed, 0)
    upper, inverse1 = advance(upper, False, keep(1), at_hi, at_lo, mixed, 1)
    l_out[...] = upper

    @pl.when(has_next)
    def _():
        along.start()

    across = pltpu.make_async_remote_copy(
        src_ref=out.at[1 - core], dst_ref=out_ref.at[0, core, 0], send_sem=out_send, recv_sem=out_recv,
        device_id=(partner, z), device_id_type=MESH,
    )
    home = pltpu.make_async_copy(out.at[core], out_ref.at[0, core, 0], out_own)

    for q, inverse in ((0, inverse0), (1, inverse1)):
        results(inverse, mixed, rows, out, q)

        @pl.when(core == q)
        def _():
            home.start()

        @pl.when(core != q)
        def _():
            across.start()

    home.wait()
    across.wait()

    @pl.when(has_next)
    def _():
        along.wait_send()

    for copy in crossing:
        copy.wait_send()
    for q in range(2):
        for d in range(1, 5):
            for half in range(2):
                for way in range(2):
                    if exists(way, d, half):
                        ring(q, way, d, half).wait_send()


def sweep(ops, limits, boundaries):
    vmem = pl.BlockSpec(memory_space=pltpu.VMEM)
    anywhere = pl.BlockSpec(memory_space=pl.ANY)
    bf16, f32 = jnp.bfloat16, jnp.float32
    dma = pltpu.SemaphoreType.DMA
    return pl.pallas_call(
        sweep_kernel,
        out_shape=jax.ShapeDtypeStruct(boundaries.shape, bf16),
        in_specs=[vmem, vmem, anywhere],
        out_specs=anywhere,
        scratch_shapes=[
            pltpu.VMEM((2, 8, N, N * N), bf16),
            pltpu.VMEM((2, 8, N, N), bf16),
            pltpu.VMEM((2, 8, 128), f32),
            pltpu.VMEM((N, N * N), f32),
            pltpu.VMEM((2048, 128), f32),
            pltpu.VMEM((2, 1024, 256), bf16),
            pltpu.VMEM((2, 1024, 256), bf16),
            pltpu.VMEM((2, 256, 2048), bf16),
            pltpu.VMEM((2, N, N * N), bf16),
            pltpu.VMEM((N, 128), f32),
            pltpu.VMEM((N, 128), f32),
            pltpu.VMEM((N, 128), f32),
            dma((3,)), dma((3,)), dma((3,)),
            dma((2, 2, 4, 2)), dma((2, 2, 4, 2)),
            dma, dma, dma, dma, dma,
        ],
        compiler_params=pltpu.CompilerParams(
            collective_id=0, has_side_effects=True, vmem_limit_bytes=40 * 1024 * 1024
        ),
    )(ops, limits, boundaries)


def on_device(boundaries, row_ops, ranks):
    my_sector = lax.axis_index("sec")
    ops = lax.dynamic_slice_in_dim(row_ops, my_sector, 1, 3).reshape(2, 8, N, N)
    ops = jnp.swapaxes(ops, 2, 3)
    limits = jnp.broadcast_to(ranks.reshape(2, 1, 1).astype(jnp.float32), (2, 8, 128))
    return sweep(ops, limits, boundaries)


def solution(mesh):
    placed = (
        P("sec", None, "col", None, None),
        P(None, "col", None, None, None, None),
        P("sec", None, "col"),
    )
    return jax.shard_map(
        on_device,
        mesh=mesh,
        in_specs=placed,
        out_specs=P("sec", None, "col", None, None),
        check_vma=False,
    )
```

time: 369 us -> 263 us (0.71)
  waiting for transfers between devices: 99.4 us -> 0 us
  Pallas kernels: 223 us -> 259 us
  local copies, waits for them, and re-layouts: 26.9 us -> 3.19 us
  between operations: 13.4 us -> 0.03 us
  matrix products: 6.37 us -> 0 us
    all_gather x1 -> x0, waiting for transfers between devices: 98.7 us -> none  [on_device(): lax.all_gather(boundaries, 'sec', axis=0, tiled=True)]
    pallas_call x1, Pallas kernels: 223 us -> 259 us  [sweep(): pl.pallas_call(sweep_kernel, out_shape=jax.ShapeDtypeStruct(boundaries.sh...]
    transpose x3 -> x0, local copies, waits for them, and re-layouts: 14 us -> none  [the longest x2 9.86 us: on_device(): absorbed.reshape(2, 16, 4, N, N).transpose(0, 1, 4, 2, 3)]
    reshape x3 -> x0, local copies, waits for them, and re-layouts: 11.3 us -> none  [the longest x1 5.28 us: on_device(): absorbed.reshape(2, 16, 4, N, N).transpose(0, 1, 4, 2, 3)]
    dot_general x1 -> x0, matrix products: 6.37 us -> none  [on_device(): jnp.einsum('sbcpx,bcstpq->tbcqx', lax.all_gather(boundaries, 'sec', axis=...]
  transfers between devices with their start and end apart: 1 -> 0, of which waited for: 1 -> 0; matrix products, arithmetic and copies ran while one was open for 0% -> 0% of each run, Pallas kernels for 0% -> 0%
where the time goes in v2:
time: 263 us
  Pallas kernels  259 us (98%)
  local copies, waits for them, and re-layouts  3.19 us (1%)
    pallas_call x1, Pallas kernels, sweep(): pl.pallas_call(sweep_kernel, out_shape=jax.ShapeDtypeStruct(boundaries.sh...  259 us

profile of v2, /device:TPU:31, one launch (start us, length us, event | category | flops | bytes accessed | tf_op | source)
XLA Modules:
  0.0 262.9 jit_solution(780477589996384580)
XLA Ops:
  0.0 0.0 copy-start
  0.0 0.8 convert_bitcast_fusion
  0.8 0.1 broadcast_in_dim.2.limit_ref
  0.9 0.7 copy-done
  1.6 0.2 copy.4
  1.8 0.0 copy-start.1
  1.8 1.2 copy-done.1
  3.0 258.9 %shard_map.37 = bf16[1,2,1,64,4096]{4,3,2,1,0:T(8,128)(2,1)S(1)} custom-call(bf16[2,8,64,64]{3,2,1,0:T(8,128)(2,1)S(1)} %bitcast.5, f32[2,8,128]{2,1,0:T(8,128)S(1)} %broadcast_in_dim.2.limit_ref, bf16[1,2,1,64,4096]{4,3,2,1,0:T(8,128)(2,1)S(1)} %copy-done.1), custom_call_target="tpu_custom_call" | custom-call | tf_op jit(solution)/shard_map/pallas_call | solution.py:311
  262.0 1.0 copy.6
  (1 shorter events, 0.0 us)
Async XLA Ops:
  0.0 1.6 copy-start
  1.8 1.2 copy-start.1

commit v3 on v2

--- a/solution.py
+++ b/solution.py
@@ -24,30 +24,53 @@
     return hi, lo
 
 
-def factor_pairs(grams):
-    count = len(grams)
-    rows = [[g[8 * i : 8 * i + 8] for i in range(8)] for g, _ in grams]
-    out = [[None] * N for _ in grams]
-    wide = (8, 128)
+WIDE = (8, 128)
+
+
+def on_lines(x, i):
+    return jnp.broadcast_to(x[i : i + 1, :], WIDE)
+
+
+def on_lanes(x, i):
+    return jnp.broadcast_to(x[:, i : i + 1], WIDE)
+
+
+def factor(g, emit):
+    rows = [g[8 * i : 8 * i + 8] for i in range(8)]
+    cols = [on_lanes(rows[0], a) for a in range(8)]
     for p in range(8):
-        cols = [{} for _ in grams]
-        for n in range(count):
-            base = grams[n][1] + 8 * p
-            for r in range(p, 8):
-                cols[n][r] = [jnp.broadcast_to(rows[n][r][:, base + a : base + a + 1], wide) for a in range(8)]
+        mine, steps, done = rows[p], [], []
+        if p < 7:
+            beside = [on_lanes(rows[p + 1], 8 * p + a) for a in range(8)]
+            ahead = [on_lanes(rows[p + 1], 8 * p + 8 + a) for a in range(8)]
         for a in range(8):
-            for n in range(count):
-                pivot = jnp.broadcast_to(cols[n][p][a][a : a + 1, :], wide)
-                inverse = 1.0 / pivot
-                row = jnp.broadcast_to(rows[n][p][a : a + 1, :], wide)
-                out[n][8 * p + a] = row[0:1] * lax.rsqrt(pivot[0:1])
-                heads = [jnp.broadcast_to(cols[n][p][b][a : a + 1, :], wide) if b > a else None for b in range(8)]
-                for r in range(p, 8):
-                    times = cols[n][r][a] * inverse
-                    for b in range(a + 1, 8):
-                        cols[n][r][b] = cols[n][r][b] - times * heads[b]
-                    rows[n][r] = rows[n][r] - times * row
-    return [jnp.concatenate(o, 0) for o in out]
+            pivot = on_lines(cols[a], a)
+            inverse = 1.0 / pivot
+            row = on_lines(mine, a)
+            done.append(row[0:1] * lax.rsqrt(pivot[0:1]))
+            heads = [on_lines(cols[b], a) if b > a else None for b in range(8)]
+            times = cols[a] * inverse
+            for b in range(a + 1, 8):
+                cols[b] = cols[b] - times * heads[b]
+            mine = mine - times * row
+            if p < 7:
+                times = beside[a] * inverse
+                for b in range(a + 1, 8):
+                    beside[b] = beside[b] - times * heads[b]
+                for b in range(8):
+                    ahead[b] = ahead[b] - times * on_lines(beside[a], b)
+                rows[p + 1] = rows[p + 1] - times * row
+            steps.append((inverse, row, heads))
+        for r in range(p + 2, 8):
+            below = [on_lanes(rows[r], 8 * p + a) for a in range(8)]
+            for a, (inverse, row, heads) in enumerate(steps):
+                times = below[a] * inverse
+                for b in range(a + 1, 8):
+                    below[b] = below[b] - times * heads[b]
+                rows[r] = rows[r] - times * row
+        emit(p, jnp.concatenate(done, 0))
+        if p < 7:
+            cols = ahead
 
 
 def patterns():
@@ -73,7 +96,7 @@
     lax.fori_loop(0, 8, tile, 0)
 
 
-def to_columns(acc, rows, at_hi, at_lo, q):
+def to_columns(acc, rows, at, q):
     low = lax.broadcasted_iota(jnp.int32, (32, 128), 1) < N
     for m in range(32):
         v = acc[:, 128 * m : 128 * m + 128]
@@ -82,29 +105,24 @@
         rows[pl.ds(2 * m + 1, 32, stride=N), :] = jnp.where(low, w[0:32], v[32:64])
     for t in range(16):
         hi, lo = split(rows[128 * t : 128 * t + 128, :].T)
-        c, half = t // 2, 128 * (t % 2)
-        at_hi[q, 128 * c : 128 * c + 128, half : half + 128] = hi
-        at_lo[q, 128 * c : 128 * c + 128, half : half + 128] = lo
-
-
-def diagonal(x, y):
-    zero = jnp.zeros((N, 128), jnp.bfloat16)
-    return jnp.concatenate([jnp.concatenate([x, y, zero, zero], 0), jnp.concatenate([zero, zero, x, y], 0)], 1)
-
-
-def advance(left, unit, keep, at_hi, at_lo, mixed, q):
+        at[q, 128 * t : 128 * t + 128, 0:128] = hi
+        at[q, 128 * t : 128 * t + 128, 128:256] = lo
+
+
+def advance(left, unit, keep, at, mixed, next_left, inverses, q, begin):
     line, low, place, eye = patterns()
-    turned = pltpu.roll(left, N, 1)
-    low_hi, low_lo = split(jnp.where(low, left, 0.0))
-    high_hi, high_lo = split(jnp.where(low, 0.0, turned))
-    w_hi, w_lo = diagonal(low_hi, high_hi), diagonal(low_lo, high_lo)
-    for c in range(8):
-        a_hi = at_hi[q, 128 * c : 128 * c + 128, :]
-        a_lo = at_lo[q, 128 * c : 128 * c + 128, :]
-        x = dot(a_hi, w_hi, NT) + dot(a_lo, w_hi, NT) + dot(a_hi, w_lo, NT)
-        hi, lo = split(x)
-        mixed[q, 0:128, 256 * c : 256 * c + 256] = hi
-        mixed[q, 128:256, 256 * c : 256 * c + 256] = lo
+    both = jnp.concatenate([jnp.where(low, left, 0.0), jnp.where(low, 0.0, pltpu.roll(left, N, 1))], 0)
+    hi, lo = split(both)
+    weights = jnp.concatenate(
+        [jnp.concatenate([hi, hi], 1), jnp.concatenate([lo, jnp.zeros_like(lo)], 1)], 0
+    )
+    for t in range(0, 16, 2):
+        o = dot(at[q, 128 * t : 128 * t + 256, :], weights, NT)
+        hi, lo = split(o[:, 0:128] + o[:, 128:256])
+        for u in range(2):
+            lanes = slice(128 * (t + u), 128 * (t + u) + 128)
+            mixed[q, 0:128, lanes] = hi[128 * u : 128 * u + 128]
+            mixed[q, 128:256, lanes] = lo[128 * u : 128 * u + 128]
     y = mixed[q]
     g = dot(y, y, NT)
     g = g[0:128] + g[128:256]
@@ -113,13 +131,20 @@
     scale = lax.rsqrt(total * (1.0 / (N * N)) + 1e-06)
     scale = jnp.where(unit, jnp.ones_like(scale), scale)
     full = (g[0:N] + pltpu.roll(g[N:], N, 1)) * (scale * scale)
-    (rows,) = factor_pairs([(jnp.where(low, full, eye), 0)])
-    upper = jnp.where(jnp.logical_and(keep, place >= line), rows, 0.0)
-    inverse = jnp.where(jnp.logical_or(low, jnp.logical_not(keep)), 0.0, rows) * (scale * float(N))
-    return upper, inverse
-
-
-def results(inverse, mixed, rows, out, q):
+
+    def emit(p, rows):
+        part = slice(8 * p, 8 * p + 8)
+        upper = jnp.logical_and(low[part], place[part] >= line[part])
+        next_left[part, :] = jnp.where(jnp.logical_and(keep[part], upper), rows, 0.0)
+        inverses[q, part, :] = jnp.where(jnp.logical_or(low[part], jnp.logical_not(keep[part])), 0.0, rows) * (scale * float(N))
+        if begin is not None:
+            begin(p)
+
+    factor(jnp.where(low, full, eye), emit)
+
+
+def results(inverses, mixed, rows, out, q):
+    inverse = inverses[q]
     pair = jnp.concatenate([pltpu.roll(inverse, N, 1), inverse], 0)
     p_hi, p_lo = split(pair)
     wide = jnp.concatenate([p_hi, p_hi], 1)
@@ -139,34 +164,23 @@
 
 def sweep_kernel(
     ops_ref, limit_ref, bnd_ref, out_ref,
-    blocks, ops, limits, acc, rows, at_hi, at_lo, mixed, out, l_in, l_out, left_ref,
+    blocks, ops, limits, acc, rows, at, mixed, out, inverses, l_in, l_out, left_ref,
     part_send, part_recv, own_sem, ring_send, ring_recv, l_send, l_recv, out_send, out_recv, out_own,
 ):
     me = lax.axis_index("col")
-    last = lax.axis_size("col") - 2
+    columns = lax.axis_size("col")
     z = lax.axis_index("sec")
     size = lax.axis_size("sec")
     core = lax.rem(me, 2)
     partner = me + 1 - 2 * core
     up, down = lax.rem(z + 1, size), lax.rem(z + size - 1, size)
-    has_next = me < last
-    has_before = me >= 2
+    after, before = lax.rem(me + 2, columns), lax.rem(me + columns - 2, columns)
+    is_first = me < 2
 
     barrier = pltpu.get_barrier_semaphore()
-    for to in ((partner, z), (me, up), (me, down)):
+    for to in ((partner, z), (me, up), (me, down), (before, z)):
         pl.semaphore_signal(barrier, inc=1, device_id=to, device_id_type=MESH)
-
-    @pl.when(has_before)
-    def _():
-        pl.semaphore_signal(barrier, inc=1, device_id=(me - 2, z), device_id_type=MESH)
-
-    @pl.when(has_next)
-    def _():
-        pl.semaphore_wait(barrier, 4)
-
-    @pl.when(jnp.logical_not(has_next))
-    def _():
-        pl.semaphore_wait(barrier, 3)
+    pl.semaphore_wait(barrier, 4)
 
     def to_partner(n, source, target):
         return pltpu.make_async_remote_copy(
@@ -235,39 +249,43 @@
             begin(1)
         absorb(ops, blocks, acc, 0, sectors(d), d == 0)
     turn(1, 1)
-    to_columns(acc, rows, at_hi, at_lo, 0)
+    to_columns(acc, rows, at, 0)
     absorb(ops, blocks, acc, 1, sectors(0), True)
     absorb(ops, blocks, acc, 1, sectors(1), False)
     for d in range(2, 5):
         turn(1, d)
         absorb(ops, blocks, acc, 1, sectors(d), False)
-    to_columns(acc, rows, at_hi, at_lo, 1)
+    to_columns(acc, rows, at, 1)
 
     line, low, place, eye = patterns()
-    along = pltpu.make_async_remote_copy(
-        src_ref=l_out, dst_ref=l_in, send_sem=l_send, recv_sem=l_recv,
-        device_id=(jnp.where(has_next, me + 2, me), z), device_id_type=MESH,
-    )
-
-    @pl.when(jnp.logical_not(has_before))
+
+    def along(part, start, size):
+        return pltpu.make_async_remote_copy(
+            src_ref=l_out.at[start : start + size], dst_ref=l_in.at[start : start + size],
+            send_sem=l_send.at[part], recv_sem=l_recv.at[part], device_id=(after, z), device_id_type=MESH,
+        )
+
+    pieces = {5: along(0, 0, 48), 7: along(1, 48, 16)}
+
+    @pl.when(is_first)
     def _():
         left_ref[...] = eye
 
-    @pl.when(has_before)
+    @pl.when(jnp.logical_not(is_first))
     def _():
-        along.wait_recv()
+        for piece in pieces.values():
+            piece.wait_recv()
         left_ref[...] = l_in[...]
 
     def keep(q):
         return line.astype(jnp.float32) < limits[q, 0:1, :]
 
-    upper, inverse0 = advance(left_ref[...], jnp.logical_not(has_before), keep(0), at_hi, at_lo, mixed, 0)
-    upper, inverse1 = advance(upper, False, keep(1), at_hi, at_lo, mixed, 1)
-    l_out[...] = upper
-
-    @pl.when(has_next)
-    def _():
-        along.start()
+    def begin_piece(p):
+        if p in pieces:
+            pieces[p].start()
+
+    advance(left_ref[...], is_first, keep(0), at, mixed, left_ref, inverses, 0, None)
+    advance(left_ref[...], False, keep(1), at, mixed, l_out, inverses, 1, begin_piece)
 
     across = pltpu.make_async_remote_copy(
         src_ref=out.at[1 - core], dst_ref=out_ref.at[0, core, 0], send_sem=out_send, recv_sem=out_recv,
@@ -275,8 +293,8 @@
     )
     home = pltpu.make_async_copy(out.at[core], out_ref.at[0, core, 0], out_own)
 
-    for q, inverse in ((0, inverse0), (1, inverse1)):
-        results(inverse, mixed, rows, out, q)
+    for q in range(2):
+        results(inverses, mixed, rows, out, q)
 
         @pl.when(core == q)
         def _():
@@ -289,9 +307,13 @@
     home.wait()
     across.wait()
 
-    @pl.when(has_next)
+    for piece in pieces.values():
+        piece.wait_send()
+
+    @pl.when(is_first)
     def _():
-        along.wait_send()
+        for piece in pieces.values():
+            piece.wait_recv()
 
     for copy in crossing:
         copy.wait_send()
@@ -319,16 +341,16 @@
             pltpu.VMEM((2, 8, 128), f32),
             pltpu.VMEM((N, N * N), f32),
             pltpu.VMEM((2048, 128), f32),
-            pltpu.VMEM((2, 1024, 256), bf16),
-            pltpu.VMEM((2, 1024, 256), bf16),
+            pltpu.VMEM((2, 2048, 256), bf16),
             pltpu.VMEM((2, 256, 2048), bf16),
             pltpu.VMEM((2, N, N * N), bf16),
+            pltpu.VMEM((2, N, 128), f32),
             pltpu.VMEM((N, 128), f32),
             pltpu.VMEM((N, 128), f32),
             pltpu.VMEM((N, 128), f32),
             dma((3,)), dma((3,)), dma((3,)),
             dma((2, 2, 4, 2)), dma((2, 2, 4, 2)),
-            dma, dma, dma, dma, dma,
+            dma((2,)), dma((2,)), dma, dma, dma,
         ],
         compiler_params=pltpu.CompilerParams(
             collective_id=0, has_side_effects=True, vmem_limit_bytes=40 * 1024 * 1024

time: 263 us -> 223 us (0.85)
  Pallas kernels: 259 us -> 217 us
    pallas_call x1, Pallas kernels: 259 us -> 217 us  [sweep(): pl.pallas_call(sweep_kernel, out_shape=jax.ShapeDtypeStruct(boundaries.sh...]
where the time goes in v3:
time: 223 us; the launch traced here: 221 us
  Pallas kernels  217 us (97%)
  local copies, waits for them, and re-layouts  3.19 us (1%)
    pallas_call x1, Pallas kernels, sweep(): pl.pallas_call(sweep_kernel, out_shape=jax.ShapeDtypeStruct(boundaries.sh...  217 us

profile of v3, /device:TPU:31, one launch (start us, length us, event | category | flops | bytes accessed | tf_op | source)
XLA Modules:
  0.0 220.7 jit_solution(15010724819689714549)
XLA Ops:
  0.0 0.0 copy-start
  0.0 0.8 convert_bitcast_fusion
  0.8 0.1 broadcast_in_dim.2.limit_ref
  0.9 0.7 copy-done
  1.6 0.2 copy.4
  1.8 0.0 copy-start.1
  1.8 1.2 copy-done.1
  3.0 216.7 %shard_map.37 = bf16[1,2,1,64,4096]{4,3,2,1,0:T(8,128)(2,1)S(1)} custom-call(bf16[2,8,64,64]{3,2,1,0:T(8,128)(2,1)S(1)} %bitcast.5, f32[2,8,128]{2,1,0:T(8,128)S(1)} %broadcast_in_dim.2.limit_ref, bf16[1,2,1,64,4096]{4,3,2,1,0:T(8,128)(2,1)S(1)} %copy-done.1), custom_call_target="tpu_custom_call" | custom-call | tf_op jit(solution)/shard_map/pallas_call | solution.py:333
  219.8 1.0 copy.6
  (1 shorter events, 0.0 us)
Async XLA Ops:
  0.0 1.6 copy-start
  1.8 1.2 copy-start.1

commit v4 on v3

--- a/solution.py
+++ b/solution.py
@@ -10,6 +10,7 @@
 
 MESH = pl.DeviceIdType.MESH
 N = 64
+OWN = 1408
 NT = (((1,), (1,)), ((), ()))
 NN = (((1,), (0,)), ((), ()))
 
@@ -165,7 +166,8 @@
 def sweep_kernel(
     ops_ref, limit_ref, bnd_ref, out_ref,
     blocks, ops, limits, acc, rows, at, mixed, out, inverses, l_in, l_out, left_ref,
-    part_send, part_recv, own_sem, ring_send, ring_recv, l_send, l_recv, out_send, out_recv, out_own,
+    guests, part_send, part_recv, own_sem, ring_send, ring_recv, l_send, l_recv, out_send, out_recv, out_own,
+    gift_send, gift_recv, back_send, back_recv,
 ):
     me = lax.axis_index("col")
     columns = lax.axis_size("col")
@@ -176,11 +178,15 @@
     up, down = lax.rem(z + 1, size), lax.rem(z + size - 1, size)
     after, before = lax.rem(me + 2, columns), lax.rem(me + columns - 2, columns)
     is_first = me < 2
+    band = columns // 4
+    row = me // band
+    is_early, is_helper = row == 0, row == 3
+    peer = me + band * (3 - 2 * row)
 
     barrier = pltpu.get_barrier_semaphore()
-    for to in ((partner, z), (me, up), (me, down), (before, z)):
+    for to in ((partner, z), (me, up), (me, down), (before, z), (peer, z)):
         pl.semaphore_signal(barrier, inc=1, device_id=to, device_id_type=MESH)
-    pl.semaphore_wait(barrier, 4)
+    pl.semaphore_wait(barrier, 5)
 
     def to_partner(n, source, target):
         return pltpu.make_async_remote_copy(
@@ -201,18 +207,43 @@
     for copy in crossing + staying:
         copy.start()
 
-    def ring(q, way, d, half):
+    def ring(flow, way, d, half):
         block = lax.rem(z + size + (d - 1 if way else 1 - d), size)
-        part = blocks.at[q, block, 32 * half : 32 * half + 32]
+        lines = slice(32 * half, 32 * half + 32)
+        if flow == 0:
+            part = blocks.at[0, block, lines]
+        elif flow == 1:
+            part = blocks.at[1, block, lines, 0:OWN]
+        elif flow == 2:
+            part = blocks.at[1, block, lines, OWN : N * N]
+        else:
+            part = guests.at[block, lines]
         return pltpu.make_async_remote_copy(
-            src_ref=part, dst_ref=part, send_sem=ring_send.at[q, way, d - 1, half], recv_sem=ring_recv.at[q, way, d - 1, half],
+            src_ref=part, dst_ref=part, send_sem=ring_send.at[flow, way, d - 1, half],
+            recv_sem=ring_recv.at[flow, way, d - 1, half],
             device_id=(me, down if way else up), device_id_type=MESH,
         )
 
-    def exists(way, d, half):
-        return d < 4 or (d == 4 and half == way)
-
-    def begin(q):
+    def gift(half):
+        lines = slice(32 * half, 32 * half + 32)
+        return pltpu.make_async_remote_copy(
+            src_ref=blocks.at[1, z, lines, OWN : N * N], dst_ref=guests.at[z, lines],
+            send_sem=gift_send.at[half], recv_sem=gift_recv.at[half], device_id=(peer, z), device_id_type=MESH,
+        )
+
+    def back(way, d, half):
+        block = lax.rem(z + size + (d if way else -d), size)
+        lines = slice(32 * half, 32 * half + 32)
+        return pltpu.make_async_remote_copy(
+            src_ref=guests.at[block, lines], dst_ref=blocks.at[1, block, lines, OWN : N * N],
+            send_sem=back_send.at[way, d - 1, half], recv_sem=back_recv.at[way, d - 1, half],
+            device_id=(peer, z), device_id_type=MESH,
+        )
+
+    def parts(d):
+        return [(way, d, half) for half in range(2) for way in range(2) if d < 4 or half == way]
+
+    def ready(q):
         @pl.when(core == q)
         def _():
             staying[0].wait()
@@ -221,23 +252,52 @@
         def _():
             crossing[0].wait_recv()
 
-        for half in range(2):
-            for way in range(2):
-                ring(q, way, 1, half).start()
-
-    def turn(q, d):
-        for half in range(2):
-            for way in range(2):
-                if exists(way, d, half):
-                    ring(q, way, d, half).wait_recv()
-                    if exists(way, d + 1, half):
-                        ring(q, way, d + 1, half).start()
+    def begin(flow):
+        for part in parts(1):
+            ring(flow, *part).start()
+
+    def turn(flow, d, then=None):
+        for way, _, half in parts(d):
+            ring(flow, way, d, half).wait_recv()
+            if (way, d + 1, half) in parts(d + 1) and d < 4:
+                ring(flow, way, d + 1, half).start()
+            if then is not None:
+                then(way, d, half).start()
+
+    def turn_second(d):
+        turn(1, d)
+
+        @pl.when(is_early)
+        def _():
+            for part in parts(d):
+                back(*part).wait_recv()
+
+        @pl.when(jnp.logical_not(is_early))
+        def _():
+            turn(2, d)
 
     def sectors(d):
         before, after = lax.rem(z + size - d, size), lax.rem(z + d, size)
         return [z] if d == 0 else [after] if d == 4 else [before, after]
 
+    @pl.when(is_helper)
+    def _():
+        for half in range(2):
+            gift(half).wait_recv()
+            for way in range(2):
+                ring(3, way, 1, half).start()
+        for d in range(1, 5):
+            turn(3, d, back)
+
+    ready(0)
     begin(0)
+    ready(1)
+
+    @pl.when(is_early)
+    def _():
+        for half in range(2):
+            gift(half).start()
+
     for copy in staying[1:]:
         copy.wait()
     for copy in crossing[1:]:
@@ -247,13 +307,18 @@
             turn(0, d)
         if d == 3:
             begin(1)
+
+            @pl.when(jnp.logical_not(is_early))
+            def _():
+                begin(2)
+
         absorb(ops, blocks, acc, 0, sectors(d), d == 0)
-    turn(1, 1)
+    turn_second(1)
     to_columns(acc, rows, at, 0)
     absorb(ops, blocks, acc, 1, sectors(0), True)
     absorb(ops, blocks, acc, 1, sectors(1), False)
     for d in range(2, 5):
-        turn(1, d)
+        turn_second(d)
         absorb(ops, blocks, acc, 1, sectors(d), False)
     to_columns(acc, rows, at, 1)
 
@@ -317,12 +382,26 @@
 
     for copy in crossing:
         copy.wait_send()
-    for q in range(2):
-        for d in range(1, 5):
-            for half in range(2):
-                for way in range(2):
-                    if exists(way, d, half):
-                        ring(q, way, d, half).wait_send()
+    every = [part for d in range(1, 5) for part in parts(d)]
+    for part in every:
+        ring(0, *part).wait_send()
+        ring(1, *part).wait_send()
+
+    @pl.when(is_early)
+    def _():
+        for half in range(2):
+            gift(half).wait_send()
+
+    @pl.when(jnp.logical_not(is_early))
+    def _():
+        for part in every:
+            ring(2, *part).wait_send()
+
+    @pl.when(is_helper)
+    def _():
+        for part in every:
+            ring(3, *part).wait_send()
+            back(*part).wait_send()
 
 
 def sweep(ops, limits, boundaries):
@@ -348,9 +427,11 @@
             pltpu.VMEM((N, 128), f32),
             pltpu.VMEM((N, 128), f32),
             pltpu.VMEM((N, 128), f32),
+            pltpu.VMEM((8, N, N * N - OWN), bf16),
             dma((3,)), dma((3,)), dma((3,)),
-            dma((2, 2, 4, 2)), dma((2, 2, 4, 2)),
+            dma((4, 2, 4, 2)), dma((4, 2, 4, 2)),
             dma((2,)), dma((2,)), dma, dma, dma,
+            dma((2,)), dma((2,)), dma((2, 4, 2)), dma((2, 4, 2)),
         ],
         compiler_params=pltpu.CompilerParams(
             collective_id=0, has_side_effects=True, vmem_limit_bytes=40 * 1024 * 1024

time: 223 us -> 207 us (0.928)
  Pallas kernels: 217 us -> 203 us
    pallas_call x1, Pallas kernels: 217 us -> 203 us  [sweep(): pl.pallas_call(sweep_kernel, out_shape=jax.ShapeDtypeStruct(boundaries.sh...]
where the time goes in v4:
time: 207 us
  Pallas kernels  203 us (98%)
  local copies, waits for them, and re-layouts  3.19 us (2%)
    pallas_call x1, Pallas kernels, sweep(): pl.pallas_call(sweep_kernel, out_shape=jax.ShapeDtypeStruct(boundaries.sh...  203 us

profile of v4, /device:TPU:31, one launch (start us, length us, event | category | flops | bytes accessed | tf_op | source)
XLA Modules:
  0.0 206.6 jit_solution(17589898358302031912)
XLA Ops:
  0.0 0.0 copy-start
  0.0 0.8 convert_bitcast_fusion
  0.8 0.1 broadcast_in_dim.2.limit_ref
  0.9 0.7 copy-done
  1.6 0.2 copy.4
  1.8 0.0 copy-start.1
  1.8 1.2 copy-done.1
  3.0 202.6 %shard_map.37 = bf16[1,2,1,64,4096]{4,3,2,1,0:T(8,128)(2,1)S(1)} custom-call(bf16[2,8,64,64]{3,2,1,0:T(8,128)(2,1)S(1)} %bitcast.5, f32[2,8,128]{2,1,0:T(8,128)S(1)} %broadcast_in_dim.2.limit_ref, bf16[1,2,1,64,4096]{4,3,2,1,0:T(8,128)(2,1)S(1)} %copy-done.1), custom_call_target="tpu_custom_call" | custom-call | tf_op jit(solution)/shard_map/pallas_call | solution.py:412
  205.7 1.0 copy.6
  (1 shorter events, 0.0 us)
Async XLA Ops:
  0.0 1.6 copy-start
  1.8 1.2 copy-start.1

commit v5 on v4

--- a/solution.py
+++ b/solution.py
@@ -10,7 +10,9 @@
 
 MESH = pl.DeviceIdType.MESH
 N = 64
-OWN = 1408
+OWN = 512
+CHUNK = 896
+MIDDLE = OWN + 2 * CHUNK
 NT = (((1,), (1,)), ((), ()))
 NN = (((1,), (0,)), ((), ()))
 
@@ -83,18 +85,17 @@
     return line, low, place, eye
 
 
-def absorb(ops, blocks, acc, q, sectors, first):
-    lhs = [ops[q, s] for s in sectors]
-
+def absorb(lefts, rights, acc, start, width, tiles, first):
     def tile(n, carry):
-        at = pl.ds(pl.multiple_of(n * 512, 512), 512)
-        total = dot(lhs[0], blocks[q, sectors[0], :, at], NN)
-        for left, s in zip(lhs[1:], sectors[1:]):
-            total = total + dot(left, blocks[q, s, :, at], NN)
+        at = pl.ds(pl.multiple_of(start + n * width, 128), width)
+        total = sum(dot(left, right[:, at], NN) for left, right in zip(lefts, rights))
         acc[:, at] = total if first else acc[:, at] + total
         return carry
 
-    lax.fori_loop(0, 8, tile, 0)
+    if tiles == 1:
+        tile(0, 0)
+    else:
+        lax.fori_loop(0, tiles, tile, 0)
 
 
 def to_columns(acc, rows, at, q):
@@ -130,7 +131,7 @@
     g = g[:, 0:128] + g[:, 128:256]
     total = jnp.sum(jnp.where(low, left * left, 0.0), keepdims=True)
     scale = lax.rsqrt(total * (1.0 / (N * N)) + 1e-06)
-    scale = jnp.where(unit, jnp.ones_like(scale), scale)
+    scale = jnp.ones_like(scale) if unit else scale
     full = (g[0:N] + pltpu.roll(g[N:], N, 1)) * (scale * scale)
 
     def emit(p, rows):
@@ -165,9 +166,9 @@
 
 def sweep_kernel(
     ops_ref, limit_ref, bnd_ref, out_ref,
-    blocks, ops, limits, acc, rows, at, mixed, out, inverses, l_in, l_out, left_ref,
-    guests, part_send, part_recv, own_sem, ring_send, ring_recv, l_send, l_recv, out_send, out_recv, out_own,
-    gift_send, gift_recv, back_send, back_recv,
+    blocks, ops, limits, acc, second, rows, at, mixed, out, inverses, l_in, l_out, left_ref,
+    guests, guest_ops, guest_sums, part_send, part_recv, own_sem, ring_send, ring_recv, l_send, l_recv, out_send, out_recv, out_own,
+    gift_send, gift_recv, back_send, back_recv, lent_send, lent_recv,
 ):
     me = lax.axis_index("col")
     columns = lax.axis_size("col")
@@ -180,7 +181,6 @@
     is_first = me < 2
     band = columns // 4
     row = me // band
-    is_early, is_helper = row == 0, row == 3
     peer = me + band * (3 - 2 * row)
 
     barrier = pltpu.get_barrier_semaphore()
@@ -207,37 +207,46 @@
     for copy in crossing + staying:
         copy.start()
 
+    edges = {1: (0, OWN), 2: (OWN, MIDDLE), 3: (MIDDLE, N * N)}
+
+    def chunk(c):
+        return slice(CHUNK * c, CHUNK * c + CHUNK)
+
+    def far_chunk(c):
+        return slice(OWN + CHUNK * c, OWN + CHUNK * c + CHUNK)
+
     def ring(flow, way, d, half):
         block = lax.rem(z + size + (d - 1 if way else 1 - d), size)
         lines = slice(32 * half, 32 * half + 32)
         if flow == 0:
             part = blocks.at[0, block, lines]
-        elif flow == 1:
-            part = blocks.at[1, block, lines, 0:OWN]
-        elif flow == 2:
-            part = blocks.at[1, block, lines, OWN : N * N]
+        elif flow < 4:
+            part = blocks.at[1, block, lines, edges[flow][0] : edges[flow][1]]
         else:
-            part = guests.at[block, lines]
+            part = guests.at[block, lines, chunk(flow - 4)]
         return pltpu.make_async_remote_copy(
             src_ref=part, dst_ref=part, send_sem=ring_send.at[flow, way, d - 1, half],
             recv_sem=ring_recv.at[flow, way, d - 1, half],
             device_id=(me, down if way else up), device_id_type=MESH,
         )
 
-    def gift(half):
+    def gift(c, half):
         lines = slice(32 * half, 32 * half + 32)
         return pltpu.make_async_remote_copy(
-            src_ref=blocks.at[1, z, lines, OWN : N * N], dst_ref=guests.at[z, lines],
-            send_sem=gift_send.at[half], recv_sem=gift_recv.at[half], device_id=(peer, z), device_id_type=MESH,
+            src_ref=blocks.at[1, z, lines, far_chunk(c)], dst_ref=guests.at[z, lines, chunk(c)],
+            send_sem=gift_send.at[c, half], recv_sem=gift_recv.at[c, half],
+            device_id=(peer, z), device_id_type=MESH,
         )
 
-    def back(way, d, half):
-        block = lax.rem(z + size + (d if way else -d), size)
-        lines = slice(32 * half, 32 * half + 32)
+    lent = pltpu.make_async_remote_copy(
+        src_ref=ops.at[1], dst_ref=guest_ops, send_sem=lent_send, recv_sem=lent_recv,
+        device_id=(peer, z), device_id_type=MESH,
+    )
+
+    def back(c):
         return pltpu.make_async_remote_copy(
-            src_ref=guests.at[block, lines], dst_ref=blocks.at[1, block, lines, OWN : N * N],
-            send_sem=back_send.at[way, d - 1, half], recv_sem=back_recv.at[way, d - 1, half],
-            device_id=(peer, z), device_id_type=MESH,
+            src_ref=guest_sums.at[:, chunk(c)], dst_ref=second.at[:, far_chunk(c)],
+            send_sem=back_send.at[c], recv_sem=back_recv.at[c], device_id=(peer, z), device_id_type=MESH,
         )
 
     def parts(d):
@@ -256,71 +265,123 @@
         for part in parts(1):
             ring(flow, *part).start()
 
-    def turn(flow, d, then=None):
+    def turn(flow, d):
         for way, _, half in parts(d):
             ring(flow, way, d, half).wait_recv()
-            if (way, d + 1, half) in parts(d + 1) and d < 4:
+            if d < 4 and (way, d + 1, half) in parts(d + 1):
                 ring(flow, way, d + 1, half).start()
-            if then is not None:
-                then(way, d, half).start()
-
-    def turn_second(d):
-        turn(1, d)
-
-        @pl.when(is_early)
-        def _():
-            for part in parts(d):
-                back(*part).wait_recv()
-
-        @pl.when(jnp.logical_not(is_early))
-        def _():
-            turn(2, d)
 
     def sectors(d):
         before, after = lax.rem(z + size - d, size), lax.rem(z + d, size)
         return [z] if d == 0 else [after] if d == 4 else [before, after]
 
-    @pl.when(is_helper)
-    def _():
+    def absorb_flow(flow, d):
+        q = 0 if flow == 0 else 1
+        start, width, tiles = {0: (0, 512, 8), 1: (0, 512, 1), 2: (OWN, 256, 7), 3: (MIDDLE, 256, 7)}[flow]
+        absorb(
+            [ops[q, s] for s in sectors(d)], [blocks.at[q, s] for s in sectors(d)],
+            second if q else acc, start, width, tiles, d == 0,
+        )
+
+    def open_guest(c):
         for half in range(2):
-            gift(half).wait_recv()
+            gift(c, half).wait_recv()
             for way in range(2):
-                ring(3, way, 1, half).start()
+                ring(4 + c, way, 1, half).start()
+
+    def serve(c, then):
         for d in range(1, 5):
-            turn(3, d, back)
+            turn(4 + c, d)
+            if d == 3:
+                then()
+        if c == 0:
+            lent.wait_recv()
+        lefts = [guest_ops[s] for s in range(8)]
+        rights = [guests.at[s] for s in range(8)]
+        for start, width in ((0, 256), (256, 256), (512, 256), (768, 128)):
+            absorb(lefts, rights, guest_sums, CHUNK * c + start, width, 1, True)
+        back(c).start()
+
+    def if_last_row(do):
+        def run():
+            @pl.when(row == 3)
+            def _():
+                do()
+
+        return run
+
+    def nothing():
+        pass
+
+    @pl.when(row >= 2)
+    def _():
+        open_guest(0)
+        serve(0, lambda: open_guest(1))
+        serve(1, if_last_row(lambda: open_guest(2)))
+
+    @pl.when(row == 3)
+    def _():
+        serve(2, lambda: open_guest(3))
+        serve(3, nothing)
 
     ready(0)
     begin(0)
     ready(1)
 
-    @pl.when(is_early)
-    def _():
-        for half in range(2):
-            gift(half).start()
+    @pl.when(row < 2)
+    def _():
+        for c in range(2):
+            for half in range(2):
+                gift(c, half).start()
+
+    @pl.when(row == 0)
+    def _():
+        for c in range(2, 4):
+            for half in range(2):
+                gift(c, half).start()
 
     for copy in staying[1:]:
         copy.wait()
     for copy in crossing[1:]:
         copy.wait_recv()
+
+    @pl.when(row < 2)
+    def _():
+        lent.start()
+
     for d in range(5):
         if d > 0:
             turn(0, d)
         if d == 3:
             begin(1)
 
-            @pl.when(jnp.logical_not(is_early))
+            @pl.when(row >= 2)
             def _():
                 begin(2)
 
-        absorb(ops, blocks, acc, 0, sectors(d), d == 0)
-    turn_second(1)
-    to_columns(acc, rows, at, 0)
-    absorb(ops, blocks, acc, 1, sectors(0), True)
-    absorb(ops, blocks, acc, 1, sectors(1), False)
-    for d in range(2, 5):
-        turn_second(d)
-        absorb(ops, blocks, acc, 1, sectors(d), False)
-    to_columns(acc, rows, at, 1)
+            @pl.when(row >= 1)
+            def _():
+                begin(3)
+
+        absorb_flow(0, d)
+    for d in range(5):
+        if d > 0:
+            turn(1, d)
+        if d == 1:
+            to_columns(acc, rows, at, 0)
+        absorb_flow(1, d)
+
+        @pl.when(row >= 2)
+        def _():
+            if d > 0:
+                turn(2, d)
+            absorb_flow(2, d)
+
+        @pl.when(row >= 1)
+        def _():
+            if d > 0:
+                turn(3, d)
+            absorb_flow(3, d)
 
     line, low, place, eye = patterns()
 
@@ -330,17 +391,7 @@
             send_sem=l_send.at[part], recv_sem=l_recv.at[part], device_id=(after, z), device_id_type=MESH,
         )
 
-    pieces = {5: along(0, 0, 48), 7: along(1, 48, 16)}
-
-    @pl.when(is_first)
-    def _():
-        left_ref[...] = eye
-
-    @pl.when(jnp.logical_not(is_first))
-    def _():
-        for piece in pieces.values():
-            piece.wait_recv()
-        left_ref[...] = l_in[...]
+    pieces = {3: along(0, 0, 32), 5: along(1, 32, 16), 6: along(2, 48, 8), 7: along(3, 56, 8)}
 
     def keep(q):
         return line.astype(jnp.float32) < limits[q, 0:1, :]
@@ -349,7 +400,28 @@
         if p in pieces:
             pieces[p].start()
 
-    advance(left_ref[...], is_first, keep(0), at, mixed, left_ref, inverses, 0, None)
+    @pl.when(is_first)
+    def _():
+        advance(eye, True, keep(0), at, mixed, left_ref, inverses, 0, None)
+
+    @pl.when(row < 2)
+    def _():
+        for c in range(2):
+            back(c).wait_recv()
+
+    @pl.when(row == 0)
+    def _():
+        for c in range(2, 4):
+            back(c).wait_recv()
+
+    to_columns(second, rows, at, 1)
+
+    @pl.when(jnp.logical_not(is_first))
+    def _():
+        for piece in pieces.values():
+            piece.wait_recv()
+        advance(l_in[...], False, keep(0), at, mixed, left_ref, inverses, 0, None)
+
     advance(left_ref[...], False, keep(1), at, mixed, l_out, inverses, 1, begin_piece)
 
     across = pltpu.make_async_remote_copy(
@@ -383,25 +455,42 @@
     for copy in crossing:
         copy.wait_send()
     every = [part for d in range(1, 5) for part in parts(d)]
-    for part in every:
-        ring(0, *part).wait_send()
-        ring(1, *part).wait_send()
-
-    @pl.when(is_early)
-    def _():
-        for half in range(2):
-            gift(half).wait_send()
-
-    @pl.when(jnp.logical_not(is_early))
-    def _():
-        for part in every:
-            ring(2, *part).wait_send()
-
-    @pl.when(is_helper)
-    def _():
-        for part in every:
-            ring(3, *part).wait_send()
-            back(*part).wait_send()
+
+    def sent(*flows):
+        for flow in flows:
+            for part in every:
+                ring(flow, *part).wait_send()
+
+    sent(0, 1)
+
+    @pl.when(row >= 2)
+    def _():
+        sent(2, 4, 5)
+        for c in range(2):
+            back(c).wait_send()
+
+    @pl.when(row >= 1)
+    def _():
+        sent(3)
+
+    @pl.when(row == 3)
+    def _():
+        sent(6, 7)
+        for c in range(2, 4):
+            back(c).wait_send()
+
+    @pl.when(row < 2)
+    def _():
+        lent.wait_send()
+        for c in range(2):
+            for half in range(2):
+                gift(c, half).wait_send()
+
+    @pl.when(row == 0)
+    def _():
+        for c in range(2, 4):
+            for half in range(2):
+                gift(c, half).wait_send()
 
 
 def sweep(ops, limits, boundaries):
@@ -419,6 +508,7 @@
             pltpu.VMEM((2, 8, N, N), bf16),
             pltpu.VMEM((2, 8, 128), f32),
             pltpu.VMEM((N, N * N), f32),
+            pltpu.VMEM((N, N * N), f32),
             pltpu.VMEM((2048, 128), f32),
             pltpu.VMEM((2, 2048, 256), bf16),
             pltpu.VMEM((2, 256, 2048), bf16),
@@ -427,11 +517,13 @@
             pltpu.VMEM((N, 128), f32),
             pltpu.VMEM((N, 128), f32),
             pltpu.VMEM((N, 128), f32),
-            pltpu.VMEM((8, N, N * N - OWN), bf16),
+            pltpu.VMEM((8, N, 4 * CHUNK), bf16),
+            pltpu.VMEM((8, N, N), bf16),
+            pltpu.VMEM((N, 4 * CHUNK), f32),
             dma((3,)), dma((3,)), dma((3,)),
-            dma((4, 2, 4, 2)), dma((4, 2, 4, 2)),
-            dma((2,)), dma((2,)), dma, dma, dma,
-            dma((2,)), dma((2,)), dma((2, 4, 2)), dma((2, 4, 2)),
+            dma((8, 2, 4, 2)), dma((8, 2, 4, 2)),
+            dma((4,)), dma((4,)), dma, dma, dma,
+            dma((4, 2)), dma((4, 2)), dma((4,)), dma((4,)), dma, dma,
         ],
         compiler_params=pltpu.CompilerParams(
             collective_id=0, has_side_effects=True, vmem_limit_bytes=40 * 1024 * 1024

time: 207 us -> 203 us (0.981)
  Pallas kernels: 203 us -> 198 us
    pallas_call x1, Pallas kernels: 203 us -> 198 us  [sweep(): pl.pallas_call(sweep_kernel, out_shape=jax.ShapeDtypeStruct(boundaries.sh...]
where the time goes in v5:
time: 203 us; the launch traced here: 202 us
  Pallas kernels  198 us (98%)
  local copies, waits for them, and re-layouts  3.19 us (2%)
    pallas_call x1, Pallas kernels, sweep(): pl.pallas_call(sweep_kernel, out_shape=jax.ShapeDtypeStruct(boundaries.sh...  198 us

profile of v5, /device:TPU:31, one launch (start us, length us, event | category | flops | bytes accessed | tf_op | source)
XLA Modules:
  0.0 201.6 jit_solution(5448197178185941110)
XLA Ops:
  0.0 0.0 copy-start
  0.0 0.8 convert_bitcast_fusion
  0.8 0.1 broadcast_in_dim.2.limit_ref
  0.9 0.7 copy-done
  1.6 0.2 copy.4
  1.8 0.0 copy-start.1
  1.8 1.2 copy-done.1
  3.0 197.5 %shard_map.37 = bf16[1,2,1,64,4096]{4,3,2,1,0:T(8,128)(2,1)S(1)} custom-call(bf16[2,8,64,64]{3,2,1,0:T(8,128)(2,1)S(1)} %bitcast.5, f32[2,8,128]{2,1,0:T(8,128)S(1)} %broadcast_in_dim.2.limit_ref, bf16[1,2,1,64,4096]{4,3,2,1,0:T(8,128)(2,1)S(1)} %copy-done.1), custom_call_target="tpu_custom_call" | custom-call | tf_op jit(solution)/shard_map/pallas_call | solution.py:501
  200.6 1.0 copy.6
  (1 shorter events, 0.0 us)
Async XLA Ops:
  0.0 1.6 copy-start
  1.8 1.2 copy-start.1

commit v6 on v5

--- a/solution.py
+++ b/solution.py
@@ -168,7 +168,7 @@
     ops_ref, limit_ref, bnd_ref, out_ref,
     blocks, ops, limits, acc, second, rows, at, mixed, out, inverses, l_in, l_out, left_ref,
     guests, guest_ops, guest_sums, part_send, part_recv, own_sem, ring_send, ring_recv, l_send, l_recv, out_send, out_recv, out_own,
-    gift_send, gift_recv, back_send, back_recv, lent_send, lent_recv,
+    gift_send, gift_recv, back_send, back_recv, lent_send, lent_recv, hop_send,
 ):
     me = lax.axis_index("col")
     columns = lax.axis_size("col")
@@ -184,9 +184,13 @@
     peer = me + band * (3 - 2 * row)
 
     barrier = pltpu.get_barrier_semaphore()
-    for to in ((partner, z), (me, up), (me, down), (before, z), (peer, z)):
+    peer_partner = peer + 1 - 2 * core
+    greeted = (
+        (partner, z), (me, up), (me, down), (partner, up), (partner, down), (before, z), (peer, z), (peer_partner, z),
+    )
+    for to in greeted:
         pl.semaphore_signal(barrier, inc=1, device_id=to, device_id_type=MESH)
-    pl.semaphore_wait(barrier, 5)
+    pl.semaphore_wait(barrier, len(greeted))
 
     def to_partner(n, source, target):
         return pltpu.make_async_remote_copy(
@@ -230,18 +234,29 @@
             device_id=(me, down if way else up), device_id_type=MESH,
         )
 
-    def gift(c, half):
+    def first_hop(flow, way, half, b):
+        q = 0 if flow == 0 else 1
         lines = slice(32 * half, 32 * half + 32)
-        return pltpu.make_async_remote_copy(
-            src_ref=blocks.at[1, z, lines, far_chunk(c)], dst_ref=guests.at[z, lines, chunk(c)],
-            send_sem=gift_send.at[c, half], recv_sem=gift_recv.at[c, half],
-            device_id=(peer, z), device_id_type=MESH,
-        )
-
-    lent = pltpu.make_async_remote_copy(
-        src_ref=ops.at[1], dst_ref=guest_ops, send_sem=lent_send, recv_sem=lent_recv,
-        device_id=(peer, z), device_id_type=MESH,
-    )
+        lanes = slice(*edges[flow]) if flow else slice(0, N * N)
+        return pltpu.make_async_remote_copy(
+            src_ref=bnd_ref.at[0, b, 0, lines, lanes], dst_ref=blocks.at[q, z, lines, lanes],
+            send_sem=hop_send.at[flow, way, half, b], recv_sem=ring_recv.at[flow, way, 0, half],
+            device_id=(me - core + b, down if way else up), device_id_type=MESH,
+        )
+
+    def gift(c, half, b):
+        lines = slice(32 * half, 32 * half + 32)
+        return pltpu.make_async_remote_copy(
+            src_ref=bnd_ref.at[0, b, 0, lines, far_chunk(c)], dst_ref=guests.at[z, lines, chunk(c)],
+            send_sem=gift_send.at[c, half, b], recv_sem=gift_recv.at[c, half],
+            device_id=(peer - core + b, z), device_id_type=MESH,
+        )
+
+    def lent(b):
+        return pltpu.make_async_remote_copy(
+            src_ref=ops_ref.at[b], dst_ref=guest_ops, send_sem=lent_send.at[b], recv_sem=lent_recv,
+            device_id=(peer - core + b, z), device_id_type=MESH,
+        )
 
     def back(c):
         return pltpu.make_async_remote_copy(
@@ -261,9 +276,14 @@
         def _():
             crossing[0].wait_recv()
 
+    def hops():
+        return [(way, half, b) for half in range(2) for way in range(2) for b in range(2)]
+
     def begin(flow):
-        for part in parts(1):
-            ring(flow, *part).start()
+        @pl.when(core == (0 if flow == 0 else 1))
+        def _():
+            for hop in hops():
+                first_hop(flow, *hop).start()
 
     def turn(flow, d):
         for way, _, half in parts(d):
@@ -285,75 +305,79 @@
 
     def open_guest(c):
         for half in range(2):
-            gift(c, half).wait_recv()
+            gift(c, half, 0).wait_recv()
             for way in range(2):
                 ring(4 + c, way, 1, half).start()
 
-    def serve(c, then):
-        for d in range(1, 5):
-            turn(4 + c, d)
-            if d == 3:
-                then()
-        if c == 0:
-            lent.wait_recv()
-        lefts = [guest_ops[s] for s in range(8)]
-        rights = [guests.at[s] for s in range(8)]
-        for start, width in ((0, 256), (256, 256), (512, 256), (768, 128)):
-            absorb(lefts, rights, guest_sums, CHUNK * c + start, width, 1, True)
-        back(c).start()
-
-    def if_last_row(do):
-        def run():
-            @pl.when(row == 3)
-            def _():
-                do()
-
-        return run
-
-    def nothing():
-        pass
-
-    @pl.when(row >= 2)
-    def _():
+    def serve(count, at_end):
         open_guest(0)
-        serve(0, lambda: open_guest(1))
-        serve(1, if_last_row(lambda: open_guest(2)))
-
-    @pl.when(row == 3)
-    def _():
-        serve(2, lambda: open_guest(3))
-        serve(3, nothing)
-
-    ready(0)
-    begin(0)
-    ready(1)
-
-    @pl.when(row < 2)
+        open_guest(1)
+        for slot in range(1, 2 * count + 3):
+            for c in range(count):
+                d = slot - 2 * c
+                if not 1 <= d <= 4:
+                    continue
+                turn(4 + c, d)
+                if d == 3 and c + 2 < count:
+                    open_guest(c + 2)
+                if d == 3 and c == count - 1:
+                    at_end()
+                if d == 4:
+                    if c == 0:
+                        lent(0).wait_recv()
+                    lefts = [guest_ops[s] for s in range(8)]
+                    rights = [guests.at[s] for s in range(8)]
+                    for start, width in ((0, 256), (256, 256), (512, 256), (768, 128)):
+                        absorb(lefts, rights, guest_sums, CHUNK * c + start, width, 1, True)
+                    back(c).start()
+
+    def begin_own():
+        begin(0)
+        begin(1)
+
+    @pl.when(jnp.logical_and(row < 2, core == 1))
     def _():
         for c in range(2):
             for half in range(2):
-                gift(c, half).start()
-
-    @pl.when(row == 0)
+                for b in range(2):
+                    gift(c, half, b).start()
+
+    @pl.when(row < 3)
+    def _():
+        begin_own()
+
+    @pl.when(jnp.logical_and(row == 0, core == 1))
     def _():
         for c in range(2, 4):
             for half in range(2):
-                gift(c, half).start()
-
+                for b in range(2):
+                    gift(c, half, b).start()
+
+    @pl.when(jnp.logical_and(row < 2, core == 1))
+    def _():
+        for b in range(2):
+            lent(b).start()
+
+    @pl.when(row == 2)
+    def _():
+        serve(2, lambda: None)
+
+    @pl.when(row == 3)
+    def _():
+        serve(4, begin_own)
+
+    ready(0)
+    ready(1)
     for copy in staying[1:]:
         copy.wait()
     for copy in crossing[1:]:
         copy.wait_recv()
 
-    @pl.when(row < 2)
-    def _():
-        lent.start()
-
     for d in range(5):
         if d > 0:
             turn(0, d)
+            turn(1, d)
         if d == 3:
-            begin(1)
 
             @pl.when(row >= 2)
             def _():
@@ -364,12 +388,9 @@
                 begin(3)
 
         absorb_flow(0, d)
+        absorb_flow(1, d)
+    to_columns(acc, rows, at, 0)
     for d in range(5):
-        if d > 0:
-            turn(1, d)
-        if d == 1:
-            to_columns(acc, rows, at, 0)
-        absorb_flow(1, d)
 
         @pl.when(row >= 2)
         def _():
@@ -454,12 +475,18 @@
 
     for copy in crossing:
         copy.wait_send()
-    every = [part for d in range(1, 5) for part in parts(d)]
+    late = [part for d in range(2, 5) for part in parts(d)]
 
     def sent(*flows):
         for flow in flows:
-            for part in every:
+            for part in late + (parts(1) if flow > 3 else []):
                 ring(flow, *part).wait_send()
+            if flow < 4:
+
+                @pl.when(core == (0 if flow == 0 else 1))
+                def _():
+                    for hop in hops():
+                        first_hop(flow, *hop).wait_send()
 
     sent(0, 1)
 
@@ -479,18 +506,20 @@
         for c in range(2, 4):
             back(c).wait_send()
 
-    @pl.when(row < 2)
-    def _():
-        lent.wait_send()
-        for c in range(2):
-            for half in range(2):
-                gift(c, half).wait_send()
-
-    @pl.when(row == 0)
-    def _():
-        for c in range(2, 4):
-            for half in range(2):
-                gift(c, half).wait_send()
+    @pl.when(jnp.logical_and(row < 2, core == 1))
+    def _():
+        for b in range(2):
+            lent(b).wait_send()
+            for c in range(2):
+                for half in range(2):
+                    gift(c, half, b).wait_send()
+
+    @pl.when(jnp.logical_and(row == 0, core == 1))
+    def _():
+        for b in range(2):
+            for c in range(2, 4):
+                for half in range(2):
+                    gift(c, half, b).wait_send()
 
 
 def sweep(ops, limits, boundaries):
@@ -523,7 +552,7 @@
             dma((3,)), dma((3,)), dma((3,)),
             dma((8, 2, 4, 2)), dma((8, 2, 4, 2)),
             dma((4,)), dma((4,)), dma, dma, dma,
-            dma((4, 2)), dma((4, 2)), dma((4,)), dma((4,)), dma, dma,
+            dma((4, 2, 2)), dma((4, 2)), dma((4,)), dma((4,)), dma((2,)), dma, dma((4, 2, 2, 2)),
         ],
         compiler_params=pltpu.CompilerParams(
             collective_id=0, has_side_effects=True, vmem_limit_bytes=40 * 1024 * 1024

time: 203 us -> 197 us (0.970)
  Pallas kernels: 198 us -> 192 us
    pallas_call x1, Pallas kernels: 198 us -> 192 us  [sweep(): pl.pallas_call(sweep_kernel, out_shape=jax.ShapeDtypeStruct(boundaries.sh...]
where the time goes in v6:
time: 197 us; the launch traced here: 196 us
  Pallas kernels  192 us (97%)
  local copies, waits for them, and re-layouts  3.19 us (2%)
    pallas_call x1, Pallas kernels, sweep(): pl.pallas_call(sweep_kernel, out_shape=jax.ShapeDtypeStruct(boundaries.sh...  192 us

profile of v6, /device:TPU:31, one launch (start us, length us, event | category | flops | bytes accessed | tf_op | source)
XLA Modules:
  0.0 196.4 jit_solution(16751489127802726111)
XLA Ops:
  0.0 0.0 copy-start
  0.0 0.8 convert_bitcast_fusion
  0.8 0.1 broadcast_in_dim.2.limit_ref
  0.9 0.7 copy-done
  1.6 0.2 copy.4
  1.8 0.0 copy-start.1
  1.8 1.2 copy-done.1
  3.0 192.3 %shard_map.37 = bf16[1,2,1,64,4096]{4,3,2,1,0:T(8,128)(2,1)S(1)} custom-call(bf16[2,8,64,64]{3,2,1,0:T(8,128)(2,1)S(1)} %bitcast.5, f32[2,8,128]{2,1,0:T(8,128)S(1)} %broadcast_in_dim.2.limit_ref, bf16[1,2,1,64,4096]{4,3,2,1,0:T(8,128)(2,1)S(1)} %copy-done.1), custom_call_target="tpu_custom_call" | custom-call | tf_op jit(solution)/shard_map/pallas_call | solution.py:530
  195.4 1.0 copy.6
  (1 shorter events, 0.0 us)
Async XLA Ops:
  0.0 1.6 copy-start
  1.8 1.2 copy-start.1

commit v7 on v6

--- a/solution.py
+++ b/solution.py
@@ -10,8 +10,8 @@
 
 MESH = pl.DeviceIdType.MESH
 N = 64
-OWN = 512
-CHUNK = 896
+OWN = 1024
+CHUNK = 768
 MIDDLE = OWN + 2 * CHUNK
 NT = (((1,), (1,)), ((), ()))
 NN = (((1,), (0,)), ((), ()))
@@ -98,6 +98,14 @@
         lax.fori_loop(0, tiles, tile, 0)
 
 
+def flip(raw, ops):
+    def one(s, carry):
+        ops[s] = raw[s].astype(jnp.float32).T.astype(jnp.bfloat16)
+        return carry
+
+    lax.fori_loop(0, 8, one, 0)
+
+
 def to_columns(acc, rows, at, q):
     low = lax.broadcasted_iota(jnp.int32, (32, 128), 1) < N
     for m in range(32):
@@ -165,9 +173,9 @@
 
 
 def sweep_kernel(
-    ops_ref, limit_ref, bnd_ref, out_ref,
-    blocks, ops, limits, acc, second, rows, at, mixed, out, inverses, l_in, l_out, left_ref,
-    guests, guest_ops, guest_sums, part_send, part_recv, own_sem, ring_send, ring_recv, l_send, l_recv, out_send, out_recv, out_own,
+    ranks_ref, ops_ref, bnd_ref, out_ref,
+    blocks, raw, ops, ranks, limits, acc, second, rows, at, mixed, out, inverses, l_in, l_out, left_ref,
+    guests, guest_raw, guest_ops, guest_sums, part_send, part_recv, own_sem, ring_send, ring_recv, l_send, l_recv, out_send, out_recv, out_own,
     gift_send, gift_recv, back_send, back_recv, lent_send, lent_recv, hop_send,
 ):
     me = lax.axis_index("col")
@@ -183,6 +191,8 @@
     row = me // band
     peer = me + band * (3 - 2 * row)
 
+    for b in range(2):
+        ranks[b] = jnp.full((8, 128), ranks_ref[0, b, 0].astype(jnp.float32))
     barrier = pltpu.get_barrier_semaphore()
     peer_partner = peer + 1 - 2 * core
     greeted = (
@@ -200,13 +210,13 @@
 
     crossing = [
         to_partner(0, bnd_ref.at[0, 1 - core, 0], blocks.at[core, z]),
-        to_partner(1, ops_ref.at[1 - core], ops.at[core]),
-        to_partner(2, limit_ref.at[1 - core], limits.at[core]),
+        to_partner(1, ops_ref.at[1 - core, 0, :, z], raw.at[core]),
+        to_partner(2, ranks.at[1 - core], limits.at[core]),
     ]
     staying = [
         pltpu.make_async_copy(bnd_ref.at[0, core, 0], blocks.at[core, z], own_sem.at[0]),
-        pltpu.make_async_copy(ops_ref.at[core], ops.at[core], own_sem.at[1]),
-        pltpu.make_async_copy(limit_ref.at[core], limits.at[core], own_sem.at[2]),
+        pltpu.make_async_copy(ops_ref.at[core, 0, :, z], raw.at[core], own_sem.at[1]),
+        pltpu.make_async_copy(ranks.at[core], limits.at[core], own_sem.at[2]),
     ]
     for copy in crossing + staying:
         copy.start()
@@ -254,7 +264,7 @@
 
     def lent(b):
         return pltpu.make_async_remote_copy(
-            src_ref=ops_ref.at[b], dst_ref=guest_ops, send_sem=lent_send.at[b], recv_sem=lent_recv,
+            src_ref=ops_ref.at[b, 0, :, z], dst_ref=guest_raw, send_sem=lent_send.at[b], recv_sem=lent_recv,
             device_id=(peer - core + b, z), device_id_type=MESH,
         )
 
@@ -297,7 +307,7 @@
 
     def absorb_flow(flow, d):
         q = 0 if flow == 0 else 1
-        start, width, tiles = {0: (0, 512, 8), 1: (0, 512, 1), 2: (OWN, 256, 7), 3: (MIDDLE, 256, 7)}[flow]
+        start, width, tiles = {0: (0, 512, 8), 1: (0, 512, 2), 2: (OWN, 256, 6), 3: (MIDDLE, 256, 6)}[flow]
         absorb(
             [ops[q, s] for s in sectors(d)], [blocks.at[q, s] for s in sectors(d)],
             second if q else acc, start, width, tiles, d == 0,
@@ -325,10 +335,10 @@
                 if d == 4:
                     if c == 0:
                         lent(0).wait_recv()
+                        flip(guest_raw, guest_ops)
                     lefts = [guest_ops[s] for s in range(8)]
                     rights = [guests.at[s] for s in range(8)]
-                    for start, width in ((0, 256), (256, 256), (512, 256), (768, 128)):
-                        absorb(lefts, rights, guest_sums, CHUNK * c + start, width, 1, True)
+                    absorb(lefts, rights, guest_sums, CHUNK * c, 256, 3, True)
                     back(c).start()
 
     def begin_own():
@@ -372,6 +382,8 @@
         copy.wait()
     for copy in crossing[1:]:
         copy.wait_recv()
+    for q in range(2):
+        flip(raw.at[q], ops.at[q])
 
     for d in range(5):
         if d > 0:
@@ -522,19 +534,20 @@
                     gift(c, half, b).wait_send()
 
 
-def sweep(ops, limits, boundaries):
-    vmem = pl.BlockSpec(memory_space=pltpu.VMEM)
-    anywhere = pl.BlockSpec(memory_space=pl.ANY)
+def sweep(ranks, ops, boundaries):
+    anywhere = pl.BlockSpec(memory_space=pltpu.HBM)
     bf16, f32 = jnp.bfloat16, jnp.float32
     dma = pltpu.SemaphoreType.DMA
     return pl.pallas_call(
         sweep_kernel,
         out_shape=jax.ShapeDtypeStruct(boundaries.shape, bf16),
-        in_specs=[vmem, vmem, anywhere],
+        in_specs=[pl.BlockSpec(memory_space=pltpu.SMEM), anywhere, anywhere],
         out_specs=anywhere,
         scratch_shapes=[
             pltpu.VMEM((2, 8, N, N * N), bf16),
             pltpu.VMEM((2, 8, N, N), bf16),
+            pltpu.VMEM((2, 8, N, N), bf16),
+            pltpu.VMEM((2, 8, 128), f32),
             pltpu.VMEM((2, 8, 128), f32),
             pltpu.VMEM((N, N * N), f32),
             pltpu.VMEM((N, N * N), f32),
@@ -548,6 +561,7 @@
             pltpu.VMEM((N, 128), f32),
             pltpu.VMEM((8, N, 4 * CHUNK), bf16),
             pltpu.VMEM((8, N, N), bf16),
+            pltpu.VMEM((8, N, N), bf16),
             pltpu.VMEM((N, 4 * CHUNK), f32),
             dma((3,)), dma((3,)), dma((3,)),
             dma((8, 2, 4, 2)), dma((8, 2, 4, 2)),
@@ -557,15 +571,11 @@
         compiler_params=pltpu.CompilerParams(
             collective_id=0, has_side_effects=True, vmem_limit_bytes=40 * 1024 * 1024
         ),
-    )(ops, limits, boundaries)
+    )(ranks, ops, boundaries)
 
 
 def on_device(boundaries, row_ops, ranks):
-    my_sector = lax.axis_index("sec")
-    ops = lax.dynamic_slice_in_dim(row_ops, my_sector, 1, 3).reshape(2, 8, N, N)
-    ops = jnp.swapaxes(ops, 2, 3)
-    limits = jnp.broadcast_to(ranks.reshape(2, 1, 1).astype(jnp.float32), (2, 8, 128))
-    return sweep(ops, limits, boundaries)
+    return sweep(ranks, row_ops, boundaries)
 
 
 def solution(mesh):

time: 197 us -> 193 us (0.980)
  Pallas kernels: 192 us -> 188 us
    pallas_call x1, Pallas kernels: 192 us -> 188 us  [sweep(): pl.pallas_call(sweep_kernel, out_shape=jax.ShapeDtypeStruct(boundaries.sh...]
    unnamed x5 -> x6, local copies, waits for them, and re-layouts: 2.92 us -> 4.53 us
where the time goes in v7:
time: 193 us; the launch traced here: 192 us
  Pallas kernels  188 us (97%)
  local copies, waits for them, and re-layouts  4.53 us (2%)
    pallas_call x1, Pallas kernels, sweep(): pl.pallas_call(sweep_kernel, out_shape=jax.ShapeDtypeStruct(boundaries.sh...  188 us
    unnamed x6, local copies, waits for them, and re-layouts  4.53 us

profile of v7, /device:TPU:31, one launch (start us, length us, event | category | flops | bytes accessed | tf_op | source)
XLA Modules:
  0.0 192.5 jit_solution(14669887348801653323)
XLA Ops:
  0.0 0.7 copy.4.ranks_ref
  0.7 0.0 copy-start
  0.7 1.6 copy-done
  2.3 0.0 copy-start.1
  2.3 1.2 copy-done.1
  3.6 188.0 %shard_map.37 = bf16[1,2,1,64,4096]{4,3,2,1,0:T(8,128)(2,1)S(1)} custom-call(s32[1,2,1]{2,1,0:T(2,128)S(1)} %copy.4.ranks_ref, bf16[2,1,8,8,64,64]{5,4,3,2,1,0:T(8,128)(2,1)S(1)} %copy-done, bf16[1,2,1,64,4096]{4,3,2,1,0:T(8,128)(2,1)S(1)} %copy-done.1), custom_call_target="tpu_custom_call" | custom-call | tf_op jit(solution)/shard_map/pallas_call | solution.py:541
  191.5 1.0 copy.6
Async XLA Ops:
  0.7 1.6 copy-start
  2.3 1.2 copy-start.1

commit v8 on v7

--- a/solution.py
+++ b/solution.py
@@ -10,8 +10,8 @@
 
 MESH = pl.DeviceIdType.MESH
 N = 64
-OWN = 1024
-CHUNK = 768
+OWN = 512
+CHUNK = 896
 MIDDLE = OWN + 2 * CHUNK
 NT = (((1,), (1,)), ((), ()))
 NN = (((1,), (0,)), ((), ()))
@@ -195,8 +195,11 @@
         ranks[b] = jnp.full((8, 128), ranks_ref[0, b, 0].astype(jnp.float32))
     barrier = pltpu.get_barrier_semaphore()
     peer_partner = peer + 1 - 2 * core
+    beside = me + band * (1 - 2 * lax.rem(row, 2))
+    beside_partner = beside + 1 - 2 * core
     greeted = (
         (partner, z), (me, up), (me, down), (partner, up), (partner, down), (before, z), (peer, z), (peer_partner, z),
+        (beside, z), (beside_partner, z),
     )
     for to in greeted:
         pl.semaphore_signal(barrier, inc=1, device_id=to, device_id_type=MESH)
@@ -259,19 +262,20 @@
         return pltpu.make_async_remote_copy(
             src_ref=bnd_ref.at[0, b, 0, lines, far_chunk(c)], dst_ref=guests.at[z, lines, chunk(c)],
             send_sem=gift_send.at[c, half, b], recv_sem=gift_recv.at[c, half],
-            device_id=(peer - core + b, z), device_id_type=MESH,
-        )
-
-    def lent(b):
+            device_id=((beside if c == 3 else peer) - core + b, z), device_id_type=MESH,
+        )
+
+    def lent(b, to_beside):
         return pltpu.make_async_remote_copy(
-            src_ref=ops_ref.at[b, 0, :, z], dst_ref=guest_raw, send_sem=lent_send.at[b], recv_sem=lent_recv,
-            device_id=(peer - core + b, z), device_id_type=MESH,
+            src_ref=ops_ref.at[b, 0, :, z], dst_ref=guest_raw, send_sem=lent_send.at[to_beside, b], recv_sem=lent_recv,
+            device_id=((beside if to_beside else peer) - core + b, z), device_id_type=MESH,
         )
 
     def back(c):
         return pltpu.make_async_remote_copy(
             src_ref=guest_sums.at[:, chunk(c)], dst_ref=second.at[:, far_chunk(c)],
-            send_sem=back_send.at[c], recv_sem=back_recv.at[c], device_id=(peer, z), device_id_type=MESH,
+            send_sem=back_send.at[c], recv_sem=back_recv.at[c],
+            device_id=(beside if c == 3 else peer, z), device_id_type=MESH,
         )
 
     def parts(d):
@@ -307,7 +311,7 @@
 
     def absorb_flow(flow, d):
         q = 0 if flow == 0 else 1
-        start, width, tiles = {0: (0, 512, 8), 1: (0, 512, 2), 2: (OWN, 256, 6), 3: (MIDDLE, 256, 6)}[flow]
+        start, width, tiles = {0: (0, 512, 8), 1: (0, 512, 1), 2: (OWN, 256, 7), 3: (MIDDLE, 256, 7)}[flow]
         absorb(
             [ops[q, s] for s in sectors(d)], [blocks.at[q, s] for s in sectors(d)],
             second if q else acc, start, width, tiles, d == 0,
@@ -318,6 +322,17 @@
             gift(c, half, 0).wait_recv()
             for way in range(2):
                 ring(4 + c, way, 1, half).start()
+
+    def borrow():
+        lent(0, 0).wait_recv()
+        flip(guest_raw, guest_ops)
+
+    def give_back(c):
+        lefts = [guest_ops[s] for s in range(8)]
+        rights = [guests.at[s] for s in range(8)]
+        for start, width in ((0, 256), (256, 256), (512, 256), (768, 128)):
+            absorb(lefts, rights, guest_sums, CHUNK * c + start, width, 1, True)
+        back(c).start()
 
     def serve(count, at_end):
         open_guest(0)
@@ -334,12 +349,8 @@
                     at_end()
                 if d == 4:
                     if c == 0:
-                        lent(0).wait_recv()
-                        flip(guest_raw, guest_ops)
-                    lefts = [guest_ops[s] for s in range(8)]
-                    rights = [guests.at[s] for s in range(8)]
-                    absorb(lefts, rights, guest_sums, CHUNK * c, 256, 3, True)
-                    back(c).start()
+                        borrow()
+                    give_back(c)
 
     def begin_own():
         begin(0)
@@ -358,23 +369,30 @@
 
     @pl.when(jnp.logical_and(row == 0, core == 1))
     def _():
-        for c in range(2, 4):
+        for c in (3, 2):
             for half in range(2):
                 for b in range(2):
                     gift(c, half, b).start()
+        for b in range(2):
+            lent(b, 1).start()
 
     @pl.when(jnp.logical_and(row < 2, core == 1))
     def _():
         for b in range(2):
-            lent(b).start()
+            lent(b, 0).start()
+
+    @pl.when(row == 1)
+    def _():
+        open_guest(3)
 
     @pl.when(row == 2)
     def _():
-        serve(2, lambda: None)
+        open_guest(0)
+        open_guest(1)
 
     @pl.when(row == 3)
     def _():
-        serve(4, begin_own)
+        serve(3, begin_own)
 
     ready(0)
     ready(1)
@@ -387,8 +405,31 @@
 
     for d in range(5):
         if d > 0:
+            @pl.when(row == 1)
+            def _():
+                if d < 3:
+                    turn(7, 2 * d - 1)
+
             turn(0, d)
             turn(1, d)
+
+            @pl.when(row == 1)
+            def _():
+                if d < 3:
+                    turn(7, 2 * d)
+                if d == 2:
+                    borrow()
+                    give_back(3)
+
+            @pl.when(row == 2)
+            def _():
+                turn(4, d)
+                turn(5, d)
+                if d == 4:
+                    borrow()
+                    give_back(0)
+                    give_back(1)
+
         if d == 3:
 
             @pl.when(row >= 2)
@@ -514,14 +555,18 @@
 
     @pl.when(row == 3)
     def _():
-        sent(6, 7)
-        for c in range(2, 4):
-            back(c).wait_send()
+        sent(6)
+        back(2).wait_send()
+
+    @pl.when(row == 1)
+    def _():
+        sent(7)
+        back(3).wait_send()
 
     @pl.when(jnp.logical_and(row < 2, core == 1))
     def _():
         for b in range(2):
-            lent(b).wait_send()
+            lent(b, 0).wait_send()
             for c in range(2):
                 for half in range(2):
                     gift(c, half, b).wait_send()
@@ -529,6 +574,7 @@
     @pl.when(jnp.logical_and(row == 0, core == 1))
     def _():
         for b in range(2):
+            lent(b, 1).wait_send()
             for c in range(2, 4):
                 for half in range(2):
                     gift(c, half, b).wait_send()
@@ -566,10 +612,10 @@
             dma((3,)), dma((3,)), dma((3,)),
             dma((8, 2, 4, 2)), dma((8, 2, 4, 2)),
             dma((4,)), dma((4,)), dma, dma, dma,
-            dma((4, 2, 2)), dma((4, 2)), dma((4,)), dma((4,)), dma((2,)), dma, dma((4, 2, 2, 2)),
+            dma((4, 2, 2)), dma((4, 2)), dma((4,)), dma((4,)), dma((2, 2)), dma, dma((4, 2, 2, 2)),
         ],
         compiler_params=pltpu.CompilerParams(
-            collective_id=0, has_side_effects=True, vmem_limit_bytes=40 * 1024 * 1024
+            collective_id=0, has_side_effects=True, vmem_limit_bytes=60 * 1024 * 1024
         ),
     )(ranks, ops, boundaries)
 

time: 193 us -> 190 us (0.984)
  Pallas kernels: 188 us -> 186 us
    pallas_call x1, Pallas kernels: 188 us -> 186 us  [sweep(): pl.pallas_call(sweep_kernel, out_shape=jax.ShapeDtypeStruct(boundaries.sh...]
    unnamed x6 -> x2, local copies, waits for them, and re-layouts: 4.53 us -> 3.58 us
where the time goes in v8:
time: 190 us; the launch traced here: 189 us
  Pallas kernels  186 us (98%)
  local copies, waits for them, and re-layouts  3.58 us (2%)
    pallas_call x1, Pallas kernels, sweep(): pl.pallas_call(sweep_kernel, out_shape=jax.ShapeDtypeStruct(boundaries.sh...  186 us

profile of v8, /device:TPU:31, one launch (start us, length us, event | category | flops | bytes accessed | tf_op | source)
XLA Modules:
  0.0 189.2 jit_solution(17019880109906050788)
XLA Ops:
  0.0 1.3 copy.4.ranks_ref
  1.3 185.6 %shard_map.37 = bf16[1,2,1,64,4096]{4,3,2,1,0:T(8,128)(2,1)} custom-call(s32[1,2,1]{2,1,0:T(2,128)} %copy.4.ranks_ref, bf16[2,1,8,8,64,64]{5,4,3,2,1,0:T(8,128)(2,1)} %ops_ref.1, bf16[1,2,1,64,4096]{4,3,2,1,0:T(8,128)(2,1)} %bnd_ref.1), custom_call_target="tpu_custom_call" | custom-call | tf_op jit(solution)/shard_map/pallas_call | solution.py:587
  186.9 2.3 %copy.6 = bf16[1,2,1,64,4096]{4,3,2,1,0:T(8,128)(2,1)} copy(bf16[1,2,1,64,4096]{4,3,2,1,0:T(8,128)(2,1)} %shard_map.37) | data formatting | bytes 2097152

commit v9 on v8

--- a/solution.py
+++ b/solution.py
@@ -10,9 +10,9 @@
 
 MESH = pl.DeviceIdType.MESH
 N = 64
+CHUNKS = (1024, 1024, 640, 896)
 OWN = 512
-CHUNK = 896
-MIDDLE = OWN + 2 * CHUNK
+MIDDLE = OWN + CHUNKS[0] + CHUNKS[1]
 NT = (((1,), (1,)), ((), ()))
 NN = (((1,), (0,)), ((), ()))
 
@@ -192,7 +192,7 @@
     peer = me + band * (3 - 2 * row)
 
     for b in range(2):
-        ranks[b] = jnp.full((8, 128), ranks_ref[0, b, 0].astype(jnp.float32))
+        ranks[b] = jnp.full((8, 128), ranks_ref[b].astype(jnp.float32))
     barrier = pltpu.get_barrier_semaphore()
     peer_partner = peer + 1 - 2 * core
     beside = me + band * (1 - 2 * lax.rem(row, 2))
@@ -227,10 +227,10 @@
     edges = {1: (0, OWN), 2: (OWN, MIDDLE), 3: (MIDDLE, N * N)}
 
     def chunk(c):
-        return slice(CHUNK * c, CHUNK * c + CHUNK)
+        return slice(sum(CHUNKS[:c]), sum(CHUNKS[: c + 1]))
 
     def far_chunk(c):
-        return slice(OWN + CHUNK * c, OWN + CHUNK * c + CHUNK)
+        return slice(OWN + sum(CHUNKS[:c]), OWN + sum(CHUNKS[: c + 1]))
 
     def ring(flow, way, d, half):
         block = lax.rem(z + size + (d - 1 if way else 1 - d), size)
@@ -311,7 +311,7 @@
 
     def absorb_flow(flow, d):
         q = 0 if flow == 0 else 1
-        start, width, tiles = {0: (0, 512, 8), 1: (0, 512, 1), 2: (OWN, 256, 7), 3: (MIDDLE, 256, 7)}[flow]
+        start, width, tiles = {0: (0, 512, 8), 1: (0, 512, 1), 2: (OWN, 256, 8), 3: (MIDDLE, 256, 6)}[flow]
         absorb(
             [ops[q, s] for s in sectors(d)], [blocks.at[q, s] for s in sectors(d)],
             second if q else acc, start, width, tiles, d == 0,
@@ -330,8 +330,10 @@
     def give_back(c):
         lefts = [guest_ops[s] for s in range(8)]
         rights = [guests.at[s] for s in range(8)]
-        for start, width in ((0, 256), (256, 256), (512, 256), (768, 128)):
-            absorb(lefts, rights, guest_sums, CHUNK * c + start, width, 1, True)
+        wide, rest = CHUNKS[c] // 256, CHUNKS[c] % 256
+        absorb(lefts, rights, guest_sums, chunk(c).start, 256, wide, True)
+        if rest:
+            absorb(lefts, rights, guest_sums, chunk(c).stop - rest, rest, 1, True)
         back(c).start()
 
     def serve(count, at_end):
@@ -405,27 +407,32 @@
 
     for d in range(5):
         if d > 0:
-            @pl.when(row == 1)
-            def _():
-                if d < 3:
-                    turn(7, 2 * d - 1)
-
+
+            def guests_turn(step):
+                @pl.when(row == 1)
+                def _():
+                    turn(7, step)
+
+                @pl.when(row == 2)
+                def _():
+                    turn(4, step)
+                    turn(5, step)
+
+            if d < 3:
+                guests_turn(2 * d - 1)
             turn(0, d)
             turn(1, d)
-
-            @pl.when(row == 1)
-            def _():
-                if d < 3:
-                    turn(7, 2 * d)
-                if d == 2:
+            if d < 3:
+                guests_turn(2 * d)
+            if d == 2:
+
+                @pl.when(row == 1)
+                def _():
                     borrow()
                     give_back(3)
 
-            @pl.when(row == 2)
-            def _():
-                turn(4, d)
-                turn(5, d)
-                if d == 4:
+                @pl.when(row == 2)
+                def _():
                     borrow()
                     give_back(0)
                     give_back(1)
@@ -605,10 +612,10 @@
             pltpu.VMEM((N, 128), f32),
             pltpu.VMEM((N, 128), f32),
             pltpu.VMEM((N, 128), f32),
-            pltpu.VMEM((8, N, 4 * CHUNK), bf16),
+            pltpu.VMEM((8, N, sum(CHUNKS)), bf16),
             pltpu.VMEM((8, N, N), bf16),
             pltpu.VMEM((8, N, N), bf16),
-            pltpu.VMEM((N, 4 * CHUNK), f32),
+            pltpu.VMEM((N, sum(CHUNKS)), f32),
             dma((3,)), dma((3,)), dma((3,)),
             dma((8, 2, 4, 2)), dma((8, 2, 4, 2)),
             dma((4,)), dma((4,)), dma, dma, dma,
@@ -621,7 +628,7 @@
 
 
 def on_device(boundaries, row_ops, ranks):
-    return sweep(ranks, row_ops, boundaries)
+    return sweep(ranks.reshape(2), row_ops, boundaries)
 
 
 def solution(mesh):

time: 190 us -> 188 us (0.989)
  no operation moved by 1% of the time
where the time goes in v9:
time: 188 us
  Pallas kernels  186 us (99%)
  local copies, waits for them, and re-layouts  2.29 us (1%)
    pallas_call x1, Pallas kernels, sweep(): pl.pallas_call(sweep_kernel, out_shape=jax.ShapeDtypeStruct(boundaries.sh...  186 us

profile of v9, /device:TPU:31, one launch (start us, length us, event | category | flops | bytes accessed | tf_op | source)
XLA Modules:
  0.0 187.9 jit_solution(17940951824650514438)
XLA Ops:
  0.0 185.6 %shard_map.37 = bf16[1,2,1,64,4096]{4,3,2,1,0:T(8,128)(2,1)} custom-call(s32[2]{0:T(128)} %bitcast.1, bf16[2,1,8,8,64,64]{5,4,3,2,1,0:T(8,128)(2,1)} %ops_ref.1, bf16[1,2,1,64,4096]{4,3,2,1,0:T(8,128)(2,1)} %bnd_ref.1), custom_call_target="tpu_custom_call" | custom-call | tf_op jit(solution)/shard_map/pallas_call | solution.py:594
  185.6 2.3 %copy.5 = bf16[1,2,1,64,4096]{4,3,2,1,0:T(8,128)(2,1)} copy(bf16[1,2,1,64,4096]{4,3,2,1,0:T(8,128)(2,1)} %shard_map.37) | data formatting | bytes 2097152

commit v10 on v9

--- a/solution.py
+++ b/solution.py
@@ -10,8 +10,8 @@
 
 MESH = pl.DeviceIdType.MESH
 N = 64
-CHUNKS = (1024, 1024, 640, 896)
-OWN = 512
+CHUNKS = (1024, 1024, 768, 1024)
+OWN = 256
 MIDDLE = OWN + CHUNKS[0] + CHUNKS[1]
 NT = (((1,), (1,)), ((), ()))
 NN = (((1,), (0,)), ((), ()))
@@ -106,13 +106,16 @@
     lax.fori_loop(0, 8, one, 0)
 
 
-def to_columns(acc, rows, at, q):
+def spread(acc, rows, start, stop):
     low = lax.broadcasted_iota(jnp.int32, (32, 128), 1) < N
-    for m in range(32):
+    for m in range(start // 128, stop // 128):
         v = acc[:, 128 * m : 128 * m + 128]
         w = pltpu.roll(v, N, 1)
         rows[pl.ds(2 * m, 32, stride=N), :] = jnp.where(low, v[0:32], w[32:64])
         rows[pl.ds(2 * m + 1, 32, stride=N), :] = jnp.where(low, w[0:32], v[32:64])
+
+
+def to_columns(rows, at, q):
     for t in range(16):
         hi, lo = split(rows[128 * t : 128 * t + 128, :].T)
         at[q, 128 * t : 128 * t + 128, 0:128] = hi
@@ -311,7 +314,7 @@
 
     def absorb_flow(flow, d):
         q = 0 if flow == 0 else 1
-        start, width, tiles = {0: (0, 512, 8), 1: (0, 512, 1), 2: (OWN, 256, 8), 3: (MIDDLE, 256, 6)}[flow]
+        start, width, tiles = {0: (0, 512, 8), 1: (0, 256, 1), 2: (OWN, 256, 8), 3: (MIDDLE, 256, 7)}[flow]
         absorb(
             [ops[q, s] for s in sectors(d)], [blocks.at[q, s] for s in sectors(d)],
             second if q else acc, start, width, tiles, d == 0,
@@ -449,7 +452,8 @@
 
         absorb_flow(0, d)
         absorb_flow(1, d)
-    to_columns(acc, rows, at, 0)
+    spread(acc, rows, 0, N * N)
+    to_columns(rows, at, 0)
     for d in range(5):
 
         @pl.when(row >= 2)
@@ -490,12 +494,15 @@
         for c in range(2):
             back(c).wait_recv()
 
+    spread(second, rows, 0, MIDDLE)
+
     @pl.when(row == 0)
     def _():
         for c in range(2, 4):
             back(c).wait_recv()
 
-    to_columns(second, rows, at, 1)
+    spread(second, rows, MIDDLE, N * N)
+    to_columns(rows, at, 1)
 
     @pl.when(jnp.logical_not(is_first))
     def _():

time: 188 us -> 188 us (level)
  no operation moved by 1% of the time
where the time goes in v10:
time: 188 us; the launch traced here: 187 us
  Pallas kernels  185 us (98%)
  local copies, waits for them, and re-layouts  2.29 us (1%)
    pallas_call x1, Pallas kernels, sweep(): pl.pallas_call(sweep_kernel, out_shape=jax.ShapeDtypeStruct(boundaries.sh...  185 us

profile of v10, /device:TPU:31, one launch (start us, length us, event | category | flops | bytes accessed | tf_op | source)
XLA Modules:
  0.0 187.0 jit_solution(2858097280946224559)
XLA Ops:
  0.0 184.7 %shard_map.37 = bf16[1,2,1,64,4096]{4,3,2,1,0:T(8,128)(2,1)} custom-call(s32[2]{0:T(128)} %bitcast.1, bf16[2,1,8,8,64,64]{5,4,3,2,1,0:T(8,128)(2,1)} %ops_ref.1, bf16[1,2,1,64,4096]{4,3,2,1,0:T(8,128)(2,1)} %bnd_ref.1), custom_call_target="tpu_custom_call" | custom-call | tf_op jit(solution)/shard_map/pallas_call | solution.py:601
  184.7 2.3 %copy.5 = bf16[1,2,1,64,4096]{4,3,2,1,0:T(8,128)(2,1)} copy(bf16[1,2,1,64,4096]{4,3,2,1,0:T(8,128)(2,1)} %shard_map.37) | data formatting | bytes 2097152

commit v11 on v10

--- a/solution.py
+++ b/solution.py
@@ -10,7 +10,7 @@
 
 MESH = pl.DeviceIdType.MESH
 N = 64
-CHUNKS = (1024, 1024, 768, 1024)
+CHUNKS = (1152, 1152, 512, 1024)
 OWN = 256
 MIDDLE = OWN + CHUNKS[0] + CHUNKS[1]
 NT = (((1,), (1,)), ((), ()))
@@ -314,7 +314,7 @@
 
     def absorb_flow(flow, d):
         q = 0 if flow == 0 else 1
-        start, width, tiles = {0: (0, 512, 8), 1: (0, 256, 1), 2: (OWN, 256, 8), 3: (MIDDLE, 256, 7)}[flow]
+        start, width, tiles = {0: (0, 512, 8), 1: (0, 256, 1), 2: (OWN, 256, 9), 3: (MIDDLE, 256, 6)}[flow]
         absorb(
             [ops[q, s] for s in sectors(d)], [blocks.at[q, s] for s in sectors(d)],
             second if q else acc, start, width, tiles, d == 0,

time: 188 us -> 187 us (level)
  Pallas kernels: 185 us -> 183 us
where the time goes in v11:
time: 187 us; the launch traced here: 185 us
  Pallas kernels  183 us (98%)
  local copies, waits for them, and re-layouts  2.29 us (1%)
    pallas_call x1, Pallas kernels, sweep(): pl.pallas_call(sweep_kernel, out_shape=jax.ShapeDtypeStruct(boundaries.sh...  183 us

profile of v11, /device:TPU:31, one launch (start us, length us, event | category | flops | bytes accessed | tf_op | source)
XLA Modules:
  0.0 185.5 jit_solution(17663018011949116313)
XLA Ops:
  0.0 183.2 %shard_map.37 = bf16[1,2,1,64,4096]{4,3,2,1,0:T(8,128)(2,1)} custom-call(s32[2]{0:T(128)} %bitcast.1, bf16[2,1,8,8,64,64]{5,4,3,2,1,0:T(8,128)(2,1)} %ops_ref.1, bf16[1,2,1,64,4096]{4,3,2,1,0:T(8,128)(2,1)} %bnd_ref.1), custom_call_target="tpu_custom_call" | custom-call | tf_op jit(solution)/shard_map/pallas_call | solution.py:601
  183.2 2.3 %copy.5 = bf16[1,2,1,64,4096]{4,3,2,1,0:T(8,128)(2,1)} copy(bf16[1,2,1,64,4096]{4,3,2,1,0:T(8,128)(2,1)} %shard_map.37) | data formatting | bytes 2097152

commit v12 on v11

--- a/solution.py
+++ b/solution.py
@@ -10,7 +10,7 @@
 
 MESH = pl.DeviceIdType.MESH
 N = 64
-CHUNKS = (1152, 1152, 512, 1024)
+CHUNKS = (1280, 1280, 256, 1024)
 OWN = 256
 MIDDLE = OWN + CHUNKS[0] + CHUNKS[1]
 NT = (((1,), (1,)), ((), ()))
@@ -314,7 +314,7 @@
 
     def absorb_flow(flow, d):
         q = 0 if flow == 0 else 1
-        start, width, tiles = {0: (0, 512, 8), 1: (0, 256, 1), 2: (OWN, 256, 9), 3: (MIDDLE, 256, 6)}[flow]
+        start, width, tiles = {0: (0, 512, 8), 1: (0, 256, 1), 2: (OWN, 256, 10), 3: (MIDDLE, 256, 5)}[flow]
         absorb(
             [ops[q, s] for s in sectors(d)], [blocks.at[q, s] for s in sectors(d)],
             second if q else acc, start, width, tiles, d == 0,

time: 187 us -> 186 us (level)
  no operation moved by 1% of the time
where the time goes in v12:
time: 186 us; the launch traced here: 185 us
  Pallas kernels  183 us (98%)
  local copies, waits for them, and re-layouts  2.29 us (1%)
    pallas_call x1, Pallas kernels, sweep(): pl.pallas_call(sweep_kernel, out_shape=jax.ShapeDtypeStruct(boundaries.sh...  183 us

profile of v12, /device:TPU:31, one launch (start us, length us, event | category | flops | bytes accessed | tf_op | source)
XLA Modules:
  0.0 185.5 jit_solution(11307351836662500090)
XLA Ops:
  0.0 183.2 %shard_map.37 = bf16[1,2,1,64,4096]{4,3,2,1,0:T(8,128)(2,1)} custom-call(s32[2]{0:T(128)} %bitcast.1, bf16[2,1,8,8,64,64]{5,4,3,2,1,0:T(8,128)(2,1)} %ops_ref.1, bf16[1,2,1,64,4096]{4,3,2,1,0:T(8,128)(2,1)} %bnd_ref.1), custom_call_target="tpu_custom_call" | custom-call | tf_op jit(solution)/shard_map/pallas_call | solution.py:601
  183.2 2.3 %copy.5 = bf16[1,2,1,64,4096]{4,3,2,1,0:T(8,128)(2,1)} copy(bf16[1,2,1,64,4096]{4,3,2,1,0:T(8,128)(2,1)} %shard_map.37) | data formatting | bytes 2097152
